TPU v7x, 512 devices: a whole 4x8x8 slice. The times are simulated.
512 devices in a mesh: dp: 128 (over z, y, core), split: 4 (over x).
Axes of the slice: x: 4, y: 8, z: 8, core: 2. Of those that a mesh axis runs over, the one named last changes fastest.
Arguments:
- tokens: bfloat16 [65536, 1024], P(('dp', 'split')), may hold values from -6 to 6
- w_up: bfloat16 [1024, 2048], P('dp', 'split'), may hold values from -0.1875 to 0.1875
- b_up: bfloat16 [2048], P('split'), may hold values from -3 to 3
- w_down: bfloat16 [2048, 1024], P('split', 'dp'), may hold values from -0.125 to 0.125
- ln_gain: float32 [1024], replicated, may hold values from 0.5 to 2
- doc_lengths: int32 [512, 16], P(('dp', 'split')), may hold values from 1 to 64, 128 in all within a row
- pool_rows: bfloat16 [57344, 1024], P(('dp', 'split')), may hold values from -12 to 12
- cluster_ids: int32 [65536], P(('dp', 'split')), may hold values from 0 to 511, as said below
Outputs:
- best_similarity: float32 [65536], P(('dp', 'split'))
Inputs may be any that keep to these rules, and one draw needn't show every extreme that they name: `cluster_ids`: cluster c belongs to owner c mod 128. The 128 rows of one device hold at most 2 rows of the clusters of any one owner; in every draw one owner gets exactly 2 rows from every device.
All inputs are finite; a program needn't handle non-finite values.
Results may differ from a plain program's by a relative error of at most 0.00046.
Values may be sent and summed in bfloat16 or wider, within the bound.
A program may use at most 64 MiB of HBM per device.

v0:
```python
import jax
import jax.numpy as jnp
from jax import lax
from jax.sharding import PartitionSpec as P


def unit_rows(values):
    return (values * lax.rsqrt(jnp.sum(values * values, axis=1, keepdims=True) + 1e-06)).astype(
        jnp.bfloat16
    )


def expand(tok_rows, up_part, bias_part, down_part):
    pre_act = jnp.dot(
        tok_rows,
        lax.all_gather(up_part, "dp", axis=0, tiled=True),
        preferred_element_type=jnp.float32,
    )
    hidden = jax.nn.gelu(
        pre_act + bias_part.astype(jnp.float32)[None, :], approximate=False
    ).astype(jnp.bfloat16)
    down_full = lax.all_gather(down_part, "dp", axis=1, tiled=True)
    return (hidden, down_full)


def on_device(tokens, w_up, b_up, w_down, ln_gain, doc_lengths, pool_rows, cluster_ids):
    tok_count = tokens.shape[0]
    up_cols, bias_cols, down_rows = (
        lax.all_gather(w_up, "split", axis=1, tiled=True),
        lax.all_gather(b_up, "split", axis=0, tiled=True),
        lax.all_gather(w_down, "split", axis=0, tiled=True),
    )
    hidden, down_full = expand(tokens, up_cols, bias_cols, down_rows)
    ffn_out = jnp.dot(hidden, down_full, preferred_element_type=jnp.float32)
    state = tokens.astype(jnp.float32) + ffn_out
    mean_row = jnp.mean(state, axis=1, keepdims=True)
    centred = state - mean_row
    var_row = jnp.mean(centred * centred, axis=1, keepdims=True)
    normed = centred * lax.rsqrt(var_row + 1e-05) * ln_gain[None, :]
    lengths = doc_lengths[0]
    ends = jnp.cumsum(lengths)
    begins = ends - lengths
    places = jnp.arange(tok_count, dtype=jnp.int32)
    member = ((places[None, :] >= begins[:, None]) & (places[None, :] < ends[:, None])).astype(
        jnp.float32
    )
    pooled = jnp.dot(member, normed, precision=lax.Precision.HIGHEST) / lengths[:, None].astype(
        jnp.float32
    )
    emb_rows = jnp.concatenate(
        [unit_rows(pool_rows.astype(jnp.float32)), unit_rows(pooled)], axis=0
    )
    row_count = emb_rows.shape[0]
    width = emb_rows.shape[1]
    owner_count = lax.axis_size("dp")
    capacity = 2 * row_count // owner_count
    slot_count = owner_count * capacity
    owner = cluster_ids % owner_count
    label = cluster_ids // owner_count
    row_index = jnp.arange(row_count, dtype=jnp.int32)
    earlier = (owner[None, :] == owner[:, None]) & (row_index[None, :] < row_index[:, None])
    place_in = jnp.sum(earlier.astype(jnp.int32), axis=1)
    target = owner * capacity + place_in
    slot_index = jnp.arange(slot_count, dtype=jnp.int32)
    match = target[None, :] == slot_index[:, None]
    slot_row = jnp.sum(jnp.where(match, row_index[None, :], 0), axis=1)
    filled = jnp.any(match, axis=1)
    send_rows = jnp.where(filled[:, None], emb_rows[slot_row], jnp.zeros((), jnp.bfloat16)).reshape(
        owner_count, capacity, width
    )
    send_label = (
        jnp.where(filled, label[slot_row], -1).astype(jnp.bfloat16).reshape(owner_count, capacity)
    )
    got_rows, got_label = (
        lax.all_to_all(send_rows, "dp", split_axis=0, concat_axis=0, tiled=True),
        lax.all_to_all(send_label, "dp", split_axis=0, concat_axis=0, tiled=True),
    )
    held_rows = got_rows.reshape(slot_count, width)
    held_label = got_label.reshape(slot_count)
    first_place = lax.axis_index("split") * slot_count + slot_index
    start_best = jnp.full((slot_count,), -1.0, jnp.float32)
    piece_rows = lax.all_gather(held_rows, "split", axis=0, tiled=True)
    piece_label = lax.all_gather(held_label, "split", axis=0, tiled=True)
    scores = lax.dot_general(
        held_rows, piece_rows, (((1,), (1,)), ((), ())), preferred_element_type=jnp.float32
    )
    columns = jnp.arange(piece_rows.shape[0], dtype=jnp.int32)
    keep = (held_label[:, None] == piece_label[None, :]) & (
        columns[None, :] != first_place[:, None]
    )
    best = jnp.maximum(start_best, jnp.max(jnp.where(keep, scores, jnp.float32(-1.0)), axis=1))
    returned = lax.all_to_all(
        best.reshape(owner_count, capacity), "dp", split_axis=0, concat_axis=0, tiled=True
    ).reshape(slot_count)
    return returned[target]


def solution(mesh):
    placed = (
        P(("dp", "split"), None),
        P("dp", "split"),
        P("split"),
        P("split", "dp"),
        P(),
        P(("dp", "split"), None),
        P(("dp", "split"), None),
        P(("dp", "split")),
    )
    return jax.shard_map(
        on_device, mesh=mesh, in_specs=placed, out_specs=P(("dp", "split")), check_vma=False
    )
```

profile of v0, /device:TPU:1, one launch (start us, length us, event | category | flops | bytes accessed | tf_op | source)
XLA Modules:
  0.0 303.8 jit_solution(4545624040626949266)
XLA Ops:
  6.5 11.8 %all_gather.22 = bf16[8,2048]{1,0:T(8,128)(2,1)} all-gather(bf16[8,512]{1,0:T(8,128)(2,1)} %param.9), channel_id=1, replica_groups=mesh['dp'=128,'split'=4] {'split'}, dimensions={1}, use_global_device_ids=true | all-gather | bytes 40960 | tf_op jit(solution)/shard_map/all_gather | solution.py:29
  18.4 10.0 %all_gather.25 = bf16[2048,8]{0,1:T(8,128)(2,1)} all-gather(bf16[512,8]{0,1:T(8,128)(2,1)} %param.11), channel_id=1, replica_groups=mesh['dp'=128,'split'=4] {'split'}, dimensions={0}, use_global_device_ids=true | all-gather | bytes 40960 | tf_op jit(solution)/shard_map/all_gather | solution.py:31
  28.5 0.7 reshape.176
  29.2 8.1 %all-gather.1 = bf16[4,1,512]{2,1,0:T(2,128)(2,1)S(1)} all-gather(bf16[1,1,512]{2,1,0:T(2,128)(2,1)S(1)} %reshape.176), channel_id=1, replica_groups=mesh['dp'=128,'split'=4] {'split'}, dimensions={0}, use_global_device_ids=true | all-gather | bytes 5120 | tf_op jit(solution)/shard_map/all_gather | solution.py:30
  37.3 0.7 copy.15
  38.2 0.7 and_select_fusion
  39.4 1.1 fusion.46
  40.5 0.7 bitcast_convert_fusion
  41.2 0.7 bitcast_subtract_fusion
  41.9 1.0 fusion.47
  42.9 66.9 %all-gather.6.cloned.1.call-done = bf16[1024,2048]{1,0:T(8,128)(2,1)} async-done(((bf16[8,2048]{1,0:T(8,128)(2,1)}), bf16[1024,2048]{1,0:T(8,128)(2,1)}) %all-gather.6.cloned.1.call-update) | async-done | bytes 4194320 | tf_op jit(solution)/shard_map/all_gather | solution.py:16
  109.9 84.6 %all-gather.8.cloned.1.call-done = bf16[2048,1024]{0,1:T(8,128)(2,1)} async-done(((bf16[2048,8]{0,1:T(8,128)(2,1)}), bf16[2048,1024]{0,1:T(8,128)(2,1)}) %all-gather.8.cloned.1.call-update) | async-done | bytes 4194320 | tf_op jit(solution)/shard_map/all_gather | solution.py:22
  194.5 8.0 %fusion.87 = (f32[128]{0:T(128)S(1)}, f32[128,1024]{1,0:T(8,128)S(1)}) fusion(bf16[2048,1024]{0,1:T(8,128)(2,1)} %all-gather.8.cloned.1.call-done, bf16[128,1024]{1,0:T(8,128)(2,1)} %param.8, bf16[1024,2048]{1,0:T(8,128)(2,1)} %all-gather.6.cloned.1.call-done, f32[2048]{0:T(1024)S(1)} %bitcast.15), kind=kOutput, calls=%fused_computation.135 | convolution fusion | flops 1091436416 | bytes 9183744 | tf_op jit(solution)/shard_map/dot_general | solution.py:34
  202.5 0.2 multiply_reduce_fusion
  202.7 0.5 multiply_reduce_fusion.1
  203.3 1.2 gather_fusion.1
  204.7 0.6 broadcast_select_fusion
  205.3 29.7 %all_to_all.17 = bf16[128,2,1024]{2,1,0:T(2,128)(2,1)S(1)} all-to-all(bf16[128,2,1024]{2,1,0:T(2,128)(2,1)S(1)} %broadcast_select_fusion), channel_id=1, replica_groups=mesh['dp'=128,'split'=4] {'dp'}, dimensions={0} | all-to-all | bytes 1048576 | tf_op jit(solution)/shard_map/all_to_all | solution.py:75
  235.0 1.0 reshape.147
  236.0 1.9 gather_fusion
  237.9 0.8 convert_element_type.55
  238.7 5.5 %all-to-all-start = ((bf16[128,1,2]{2,1,0:T(2,128)(2,1)}), bf16[128,1,2]{2,1,0:T(2,128)(2,1)S(1)}, u32[]{:S(2)}, u32[]{:S(2)}) async-start(bf16[128,1,2]{2,1,0:T(2,128)(2,1)} %convert_element_type.55), calls=%async_computation | async-start | bytes 131072 | tf_op jit(solution)/shard_map/all_to_all | solution.py:76
  244.2 11.4 %all-to-all-done = bf16[128,1,2]{2,1,0:T(2,128)(2,1)S(1)} async-done(((bf16[128,1,2]{2,1,0:T(2,128)(2,1)}), bf16[128,1,2]{2,1,0:T(2,128)(2,1)S(1)}, u32[]{:S(2)}, u32[]{:S(2)}) %all-to-all-start) | async-done | bytes 544 | tf_op jit(solution)/shard_map/all_to_all | solution.py:76
  256.1 8.4 %all-gather = bf16[4,1,256]{2,1,0:T(2,128)(2,1)S(1)} all-gather(bf16[1,1,256]{2,1,0:T(2,128)(2,1)S(1)} %reshape.174), channel_id=1, replica_groups=mesh['dp'=128,'split'=4] {'split'}, dimensions={0}, use_global_device_ids=true | all-gather | bytes 2560 | tf_op jit(solution)/shard_map/all_gather | solution.py:83
  264.6 0.3 all-gather.10.cloned.1.call-done
  264.8 2.7 fusion
  267.5 0.8 max_broadcast_in_dim.15
  268.3 14.3 %all-to-all-start.2 = ((f32[128,1,2]{2,1,0:T(1,128)}), f32[128,1,2]{2,1,0:T(1,128)S(1)}, u32[]{:S(2)}, u32[]{:S(2)}) async-start(f32[128,1,2]{2,1,0:T(1,128)} %bitcast.5), calls=%async_computation.2 | async-start | bytes 131072 | tf_op jit(solution)/shard_map/all_to_all | solution.py:92
  282.6 11.4 %all-to-all-done.2 = f32[128,1,2]{2,1,0:T(1,128)S(1)} async-done(((f32[128,1,2]{2,1,0:T(1,128)}), f32[128,1,2]{2,1,0:T(1,128)S(1)}, u32[]{:S(2)}, u32[]{:S(2)}) %all-to-all-start.2) | async-done | bytes 1056 | tf_op jit(solution)/shard_map/all_to_all | solution.py:92
  294.0 0.5 broadcast.145
  294.5 0.8 reduce.7
  295.5 1.8 gather_fusion.2
  (35 shorter events, 1.9 us)
Async XLA Ops:
  6.5 103.3 %all-gather.6.cloned.1.call-start = ((), (), s32[]{:S(2)}) async-start(), calls=%async_computation.3 | async-start | bytes 4227072 | tf_op jit(solution)/shard_map/all_gather | solution.py:16
  18.4 176.1 %all-gather.8.cloned.1.call-start = ((), (), s32[]{:S(2)}) async-start(), calls=%async_computation.4 | async-start | bytes 4227072 | tf_op jit(solution)/shard_map/all_gather | solution.py:22
  28.5 236.4 %all-gather.10.cloned.1.call-start = ((), (), s32[]{:S(2)}) async-start(), calls=%async_computation.5 | async-start | bytes 2621440 | tf_op jit(solution)/shard_map/all_gather | solution.py:82
  194.5 8.2 %copy-start = (f32[1024]{0:T(1024)S(1)}, f32[1024]{0:T(1024)}, u32[]{:S(2)}) copy-start(f32[1024]{0:T(1024)} %param.12) | copy-start | bytes 12292
  238.7 16.9 %all-to-all-start = ((bf16[128,1,2]{2,1,0:T(2,128)(2,1)}), bf16[128,1,2]{2,1,0:T(2,128)(2,1)S(1)}, u32[]{:S(2)}, u32[]{:S(2)}) async-start(bf16[128,1,2]{2,1,0:T(2,128)(2,1)} %convert_element_type.55), calls=%async_computation | async-start | bytes 131072 | tf_op jit(solution)/shard_map/all_to_all | solution.py:76
  268.3 25.7 %all-to-all-start.2 = ((f32[128,1,2]{2,1,0:T(1,128)}), f32[128,1,2]{2,1,0:T(1,128)S(1)}, u32[]{:S(2)}, u32[]{:S(2)}) async-start(f32[128,1,2]{2,1,0:T(1,128)} %bitcast.5), calls=%async_computation.2 | async-start | bytes 131072 | tf_op jit(solution)/shard_map/all_to_all | solution.py:92
Sparse Core Ops, SparseCore 0:
  18.5 91.2 all-gather.5
  113.0 81.4 all-gather.7
  236.2 28.6 all-gather.9
where the time goes:
time: 304 us
  waiting for transfers between devices  175 us (58%)
  blocking collectives  68.1 us (22%)
  starting transfers between devices  19.9 us (7%)
  between operations  13.3 us (4%)
  matrix products  11.1 us (4%)
  local copies, waits for them, and re-layouts  10.1 us (3%)
  other arithmetic  6.65 us (2%)
    all_gather x1, waiting for transfers between devices, expand(): down_full = lax.all_gather(down_part, 'dp', axis=1, tiled=True)  84.6 us
    all_gather x1, waiting for transfers between devices, expand(): lax.all_gather(up_part, 'dp', axis=0, tiled=True)  66.9 us
    all_to_all x1, blocking collectives, on_device(): lax.all_to_all(send_rows, 'dp', split_axis=0, concat_axis=0, tiled=True)  29.7 us
    all_to_all x1, starting transfers between devices, on_device(): lax.all_to_all(best.reshape(owner_count, capacity), 'dp', split_axis=0, c...  14.3 us
    all_gather x1, blocking collectives, on_device(): lax.all_gather(w_up, 'split', axis=1, tiled=True)  11.8 us
    all_to_all x1, waiting for transfers between devices, on_device(): lax.all_to_all(best.reshape(owner_count, capacity), 'dp', split_axis=0, c...  11.4 us
    all_to_all x1, waiting for transfers between devices, on_device(): lax.all_to_all(send_label, 'dp', split_axis=0, concat_axis=0, tiled=True)  11.4 us
    all_gather x1, blocking collectives, on_device(): lax.all_gather(w_down, 'split', axis=0, tiled=True)  9.98 us
  transfers between devices with their start and end apart: 5, of which 5 were waited for; matrix products, arithmetic and copies ran while one was open for 3% of the time, Pallas kernels for 0%

commit v1 on v0

v1 whole, which is shorter than its diff:
```python
import functools
import math

import jax
import jax.numpy as jnp
from jax import lax
from jax.experimental import pallas as pl
from jax.experimental.pallas import tpu as pltpu
from jax.sharding import PartitionSpec as P

MESH = pl.DeviceIdType.MESH
F32, BF16 = jnp.float32, jnp.bfloat16
LAB = 128


def iota(shape, dim):
    return lax.broadcasted_iota(jnp.int32, shape, dim)


def mm(a, b):
    return jnp.dot(a, b, preferred_element_type=F32)


def mm_nt(a, b):
    return lax.dot_general(a, b, (((1,), (1,)), ((), ())), preferred_element_type=F32)


def unit_rows(v):
    return (v * lax.rsqrt(jnp.sum(v * v, axis=1, keepdims=True) + 1e-06)).astype(BF16)


def here(n):
    me = lax.axis_index("dp")
    return me, me // (2 * n), (me // 2) % n, me % 2, lax.axis_index("split")


def to_column(row, size):
    eye = iota((size, size), 0) == iota((size, size), 1)
    return jnp.sum(jnp.where(eye, row, 0.0), axis=1, keepdims=True)


def slots(ids_ref, n):
    dp = 2 * n * n
    rows = ids_ref.shape[1]
    ids = ids_ref[...]
    owner, label = ids & (dp - 1), ids >> int(math.log2(dp))
    owner_col = to_column(owner.astype(F32), rows)
    same = owner_col == owner.astype(F32)
    before = iota((rows, rows), 0) < iota((rows, rows), 1)
    place = jnp.sum(jnp.where(same & before, 1.0, 0.0), axis=0, keepdims=True).astype(jnp.int32)
    return owner, place, to_column(label.astype(F32), rows)


def remote(src, dst, send, recv, dev):
    return pltpu.make_async_remote_copy(
        src_ref=src, dst_ref=dst, send_sem=send, recv_sem=recv, device_id=dev, device_id_type=MESH
    )


def encode_kernel(
    n, nx, shard, tok, bias, gain, lengths, pool, ids, s0, s1,
    G, T, up, down, PS, RF, RA, emb,
    lsem, p1s, p1r, rs_, rr, sibs, sibr, ts, tr, fs, fr, qs, qr,
):
    me, z, y, c, x = here(n)
    hh = shard.shape[2]
    toks, d = tok.shape
    half = toks // 2
    xp, xm = (x + 1) % nx, (x + nx - 1) % nx
    xo = (x + 2) % nx
    place = (y, z)

    def at_z(zz):
        return ((zz * n + y) * 2 + c, x)

    def at_y(yy):
        return ((z * n + yy) * 2 + c, x)

    ring = (at_y, at_z)
    first = (at_z, at_y)
    sibling = (me + 1 - 2 * c, x)

    barrier = pltpu.get_barrier_semaphore()

    @pl.loop(1, n)
    def _(k):
        pl.semaphore_signal(barrier, 1, device_id=at_z((z + k) % n), device_id_type=MESH)
        pl.semaphore_signal(barrier, 1, device_id=at_y((y + k) % n), device_id_type=MESH)

    pl.semaphore_signal(barrier, 1, device_id=sibling, device_id_type=MESH)
    pl.semaphore_signal(barrier, 1, device_id=(me, xp), device_id_type=MESH)
    pl.semaphore_signal(barrier, 1, device_id=(me, xm), device_id_type=MESH)
    pl.semaphore_wait(barrier, 2 * (n - 1) + 3)

    lo, hi = pl.ds(0, half), pl.ds(half, half)

    own0 = pltpu.make_async_copy(shard.at[0], G.at[c, 0, y, z], lsem.at[0])
    own1 = pltpu.make_async_copy(shard.at[1], G.at[c, 1, z, y], lsem.at[1])
    own0.start()
    own1.start()

    def first_hop(h, k):
        mine = (z, y)[h]
        other = (mine + k) % n
        slot = G.at[c, 0, y, z] if h == 0 else G.at[c, 1, z, y]
        return remote(shard.at[h], slot, p1s.at[h, other], p1r.at[h, mine], first[h](other))

    @pl.loop(1, n)
    def _(k):
        first_hop(0, k).start()
        first_hop(1, k).start()

    t_send = [
        remote(tok.at[lo], T.at[x, lo], ts.at[0], tr.at[0], (me, xp)),
        remote(tok.at[hi], T.at[x, hi], ts.at[1], tr.at[1], (me, xm)),
        remote(tok.at[hi], T.at[x, hi], ts.at[2], tr.at[2], (me, xp)),
        remote(tok.at[lo], T.at[x, lo], ts.at[3], tr.at[3], (me, xm)),
    ]
    for t in t_send:
        t.start()

    pool_n = pool.shape[0]
    emb[0:pool_n, :] = unit_rows(pool[...].astype(F32))

    own0.wait()
    own1.wait()

    @pl.loop(1, n)
    def _(k):
        for h in range(2):
            mine = (z, y)[h]
            other = (mine + k) % n
            slot = G.at[c, 0, y, other] if h == 0 else G.at[c, 1, z, other]
            remote(shard.at[h], slot, p1s.at[h, other], p1r.at[h, other], first[h](other)).wait_recv()

    last = n // 2 - 1
    hops, sib = [], []

    def to_sibling(h, i, k):
        cp = remote(G.at[c, h, i], G.at[c, h, i], sibs.at[h, k], sibr.at[h, k], sibling)
        cp.start()
        sib.append(cp)

    for s in range(n // 2):
        for h in range(2):
            q = place[h]
            a, b = (q + n - s) % n, (q + s) % n
            if s:
                hops[-4 if h == 0 else -4][0].wait_recv()
                hops[-3 if h == 0 else -3][0].wait_recv()
                to_sibling(h, a, 2 * s - 1)
                to_sibling(h, b, 2 * s)
            else:
                to_sibling(h, q, 0)
            ra, rb = G.at[c, h, a], G.at[c, h, b]
            if s == last:
                ra, rb = G.at[c, h, a, pl.ds(0, n // 2)], G.at[c, h, b, pl.ds(n // 2, n // 2)]
            cp = remote(ra, ra, rs_.at[0, h, s], rr.at[0, h, s], ring[h]((q + 1) % n))
            cm = remote(rb, rb, rs_.at[1, h, s], rr.at[1, h, s], ring[h]((q + n - 1) % n))
            cp.start()
            cm.start()
            hops += [(cp,), (cm,)]

    t_send[0].wait_recv()
    f0 = remote(T.at[xm, lo], T.at[xm, lo], fs.at[0], fr.at[0], (me, xp))
    f0.start()
    t_send[1].wait_recv()
    f1 = remote(T.at[xp, hi], T.at[xp, hi], fs.at[1], fr.at[1], (me, xm))
    f1.start()

    for h in range(2):
        hops[-4 + 2 * h][0].wait_recv()
        hops[-3 + 2 * h][0].wait_recv()
        to_sibling(h, (place[h] + n // 2) % n, n - 1)

    owner, place_in, label_col = slots(ids, n)
    dp = 2 * n * n
    rows = ids.shape[1]
    lane_slot = iota((2 * dp, rows), 0)
    target0 = ((owner % (2 * n)) * n + owner // (2 * n)) * 2 + place_in
    target1 = owner * 2 + place_in
    pick0 = jnp.where(lane_slot == target0, 1.0, 0.0).astype(BF16)
    pick1 = jnp.where(lane_slot == target1, 1.0, 0.0).astype(BF16)
    lab = jnp.broadcast_to(label_col + 1.0, (rows, LAB)).astype(BF16)
    s0[:, d // 2 :] = mm(pick0, lab).astype(BF16)

    for cp in sib:
        cp.wait_recv()

    m = n * 16
    o, i_ = iota((2 * m, 2 * m), 0), iota((2 * m, 2 * m), 1)
    w_, rest = o // m, o % m
    n_, c_, r_ = rest // 16, (rest // 8) % 2, rest % 8
    order = jnp.where(i_ == c_ * m + n_ * 16 + w_ * 8 + r_, 1.0, 0.0).astype(BF16)

    @pl.loop(0, n)
    def _(i):
        for h in range(2):
            both = jnp.concatenate([G[0, h, i].reshape(m, hh), G[1, h, i].reshape(m, hh)], axis=0)
            w = mm(order, both).astype(BF16)
            cols = slice(h * hh, (h + 1) * hh)
            for ref, part in ((up, w[:m]), (down, w[m:])):
                if h == 0:
                    for zz in range(n):
                        at = pl.multiple_of((zz * n + i) * 16, 16)
                        ref[pl.ds(at, 16), cols] = part[zz * 16 : (zz + 1) * 16]
                else:
                    ref[pl.ds(pl.multiple_of(i * m, m), m), cols] = part

    def ffn(block):
        pre = mm(block, up[...]) + bias[...].astype(F32)
        hidden = (0.5 * pre * (1.0 + lax.erf(pre * (0.5**0.5)))).astype(BF16)
        return mm_nt(hidden, down[...])

    for t in t_send[2:]:
        t.wait_recv()
    f0.wait_recv()
    f1.wait_recv()
    PS[0] = ffn(T[xo]).astype(BF16)
    q0 = remote(PS.at[0, lo], RF.at[0], qs.at[0], qr.at[0], (me, xp))
    q1 = remote(PS.at[0, hi], RF.at[1], qs.at[1], qr.at[1], (me, xm))
    q0.start()
    q1.start()
    right = ffn(T[xp])
    PS[1, hi] = right[half:].astype(BF16)
    q2 = remote(PS.at[1, hi], RA.at[0, hi], qs.at[2], qr.at[2], (me, xp))
    q2.start()
    left = ffn(T[xm])
    PS[2, lo] = left[:half].astype(BF16)
    q3 = remote(PS.at[2, lo], RA.at[1, lo], qs.at[3], qr.at[3], (me, xm))
    q3.start()
    q0.wait_recv()
    PS[1, lo] = (right[:half] + RF[0].astype(F32)).astype(BF16)
    q4 = remote(PS.at[1, lo], RA.at[0, lo], qs.at[4], qr.at[4], (me, xp))
    q4.start()
    q1.wait_recv()
    PS[2, hi] = (left[half:] + RF[1].astype(F32)).astype(BF16)
    q5 = remote(PS.at[2, hi], RA.at[1, hi], qs.at[5], qr.at[5], (me, xm))
    q5.start()
    state = tok[...].astype(F32) + ffn(tok[...])
    for q in (q2, q3, q4, q5):
        q.wait_recv()
    state = state + RA[0].astype(F32) + RA[1].astype(F32)

    mean = jnp.mean(state, axis=1, keepdims=True)
    centred = state - mean
    var = jnp.mean(centred * centred, axis=1, keepdims=True)
    normed = centred * lax.rsqrt(var + 1e-05) * gain[...]
    docs = lengths.shape[1]
    len_row = lengths[...].astype(F32)
    len_col = to_column(len_row, docs)
    upto = iota((docs, docs), 1) <= iota((docs, docs), 0)
    ends = jnp.sum(jnp.where(upto, len_row, 0.0), axis=1, keepdims=True)
    places = iota((docs, toks), 1).astype(F32)
    member = jnp.where((places >= ends - len_col) & (places < ends), 1.0, 0.0)
    pooled = (
        jnp.dot(member, normed, precision=lax.Precision.HIGHEST, preferred_element_type=F32)
        / len_col
    )
    emb[pool_n : pool_n + docs, :] = unit_rows(pooled)

    s0[:, : d // 2] = mm(pick0, emb[:, : d // 2]).astype(BF16)
    s1[...] = mm(pick1, emb[:, d // 2 :]).astype(BF16)

    @pl.loop(1, n)
    def _(k):
        first_hop(0, k).wait_send()
        first_hop(1, k).wait_send()

    for cp in [*t_send, f0, f1, q0, q1, q2, q3, q4, q5, *[h[0] for h in hops], *sib]:
        cp.wait_send()


def search_kernel(
    n, nx, s0, s1, ids, out,
    R0, T0, F0, R1, T1, F1, E, LR, MX, GX, B1, B2, B3,
    lsem, s0s, s0r, s1s, s1r, t0s, t0r, t1s, t1r, es, er, ms, mr, b1s, b1r, b2s, b2r,
):
    me, z, y, c, x = here(n)
    yc = me % (2 * n)
    nyc = 2 * n
    w0 = s0.shape[2]
    w1 = s1.shape[2]
    total = 2 * nyc * n
    xp, xm = (x + 1) % nx, (x + nx - 1) % nx

    def at_z(zz):
        return (zz * nyc + yc, x)

    def at_yc(other):
        return (z * nyc + other, x)

    barrier = pltpu.get_barrier_semaphore()

    @pl.loop(1, n)
    def _(k):
        pl.semaphore_signal(barrier, 1, device_id=at_z((z + k) % n), device_id_type=MESH)

    @pl.loop(1, nyc)
    def _(k):
        pl.semaphore_signal(barrier, 1, device_id=at_yc((yc + k) % nyc), device_id_type=MESH)

    pl.semaphore_signal(barrier, 1, device_id=(me, xp), device_id_type=MESH)
    pl.semaphore_signal(barrier, 1, device_id=(me, xm), device_id_type=MESH)
    pl.semaphore_wait(barrier, n + nyc)

    def all_to_all(src, dst, mine, count, dev, send, recv, local):
        own = pltpu.make_async_copy(src.at[mine], dst.at[mine], local)

        def to(k):
            other = (mine + k) % count
            return remote(src.at[other], dst.at[mine], send.at[other], recv.at[mine], dev(other))

        def start():
            own.start()

            @pl.loop(1, count)
            def _(k):
                to(k).start()

        def wait():
            @pl.loop(1, count)
            def _(k):
                other = (mine + k) % count
                remote(src.at[other], dst.at[other], send.at[other], recv.at[other], dev(other)).wait()

            own.wait()

        return start, wait

    def spread(src, dst, mine, count, dev, send, recv, local):
        own = pltpu.make_async_copy(src, dst.at[mine], local)

        def start():
            own.start()

            @pl.loop(1, count)
            def _(k):
                other = (mine + k) % count
                remote(src, dst.at[mine], send.at[other], recv.at[mine], dev(other)).start()

        def wait():
            @pl.loop(1, count)
            def _(k):
                other = (mine + k) % count
                remote(src, dst.at[other], send.at[other], recv.at[other], dev(other)).wait()

            own.wait()

        return start, wait

    a0 = all_to_all(s0, R0, yc, nyc, at_yc, s0s, s0r, lsem.at[0])
    a1 = all_to_all(s1, R1, z, n, at_z, s1s, s1r, lsem.at[1])
    b0 = all_to_all(T0, F0, z, n, at_z, t0s, t0r, lsem.at[2])
    b1 = all_to_all(T1, F1, yc, nyc, at_yc, t1s, t1r, lsem.at[3])
    a0[0]()
    a1[0]()

    row, col = iota((total, total), 0), iota((total, total), 1)
    z_, yc_, s_ = row // (2 * nyc), (row // 2) % nyc, row % 2
    by_z = jnp.where(col == (yc_ * n + z_) * 2 + s_, 1.0, 0.0).astype(BF16)
    yc_, z_ = row // (2 * n), (row // 2) % n
    by_yc = jnp.where(col == (z_ * nyc + yc_) * 2 + s_, 1.0, 0.0).astype(BF16)

    a0[1]()
    T0[...] = mm(by_z, R0[...].reshape(total, w0)).astype(BF16).reshape(n, 2 * nyc, w0)
    b0[0]()
    a1[1]()
    T1[...] = mm(by_yc, R1[...].reshape(total, w1)).astype(BF16).reshape(nyc, 2 * n, w1)
    b1[0]()
    b0[1]()
    E[0, :, w1:] = F0[...].reshape(total, w0)
    b1[1]()
    E[0, :, :w1] = mm(by_z, F1[...].reshape(total, w1)).astype(BF16)

    to_p = remote(E.at[0], E.at[1], es.at[0], er.at[0], (me, xp))
    to_m = remote(E.at[0], E.at[2], es.at[1], er.at[1], (me, xm))
    to_p.start()
    to_m.start()

    d = w0 - LAB + w1
    eye = row == col

    def labels(i):
        col_ = E[i, :, d : d + 1].astype(F32)
        return col_, jnp.sum(jnp.where(eye, col_, 0.0), axis=0, keepdims=True)

    def best_of(rows_from, lab_col, cols_from, lab_row, self_too):
        sc = mm_nt(E[rows_from, :, :d], E[cols_from, :, :d])
        keep = lab_col == lab_row
        if self_too:
            keep = keep & ~eye
        return jnp.max(jnp.where(keep, sc, -1.0), axis=0, keepdims=True)

    col0, row0 = labels(0)
    best = best_of(0, col0, 0, row0, True)
    to_p.wait_recv()
    to_m.wait_recv()
    col1, row1 = labels(1)
    col2, _ = labels(2)
    MX[...] = jnp.broadcast_to(best_of(2, col2, 1, row1, False), MX.shape)
    mx = remote(MX, GX, ms.at[0], mr.at[0], (me, xm))
    mx.start()
    best = jnp.maximum(best, best_of(1, col1, 0, row0, False))
    best = jnp.maximum(best, best_of(2, col2, 0, row0, False))
    owner, place_in, _ = slots(ids, n)
    mx.wait_recv()
    B1[...] = jnp.broadcast_to(jnp.maximum(best, GX[0:1, :]), B1.shape)

    c1 = spread(B1.at[pl.ds(0, 1)], B2, z, n, at_z, b1s, b1r, lsem.at[4])
    c1[0]()
    c1[1]()
    LR[...] = B2[...].reshape(n, total)
    c2 = spread(LR, B3, yc, nyc, at_yc, b2s, b2r, lsem.at[5])
    c2[0]()
    c2[1]()
    got = B3[...].reshape(nyc * n, total)
    lane = iota((nyc * n, total), 1)
    v0 = jnp.sum(jnp.where(lane == me * 2, got, 0.0), axis=1, keepdims=True)
    v1 = jnp.sum(jnp.where(lane == me * 2 + 1, got, 0.0), axis=1, keepdims=True)
    rows = ids.shape[1]
    mine = iota((nyc * n, rows), 0) == (owner % nyc) * n + owner // nyc
    out[...] = jnp.sum(jnp.where(mine, jnp.where(place_in == 0, v0, v1), 0.0), axis=0, keepdims=True)
    to_p.wait_send()
    to_m.wait_send()
    mx.wait_send()


VM = pl.BlockSpec(memory_space=pltpu.VMEM)
DMA = pltpu.SemaphoreType.DMA


def on_device(n, nx, tokens, w_up, b_up, w_down, ln_gain, doc_lengths, pool_rows, cluster_ids):
    toks, d = tokens.shape
    hid = w_up.shape[1]
    hh = hid // 2
    rows = cluster_ids.shape[0]
    dp = 2 * n * n
    shard = jnp.concatenate([w_up, w_down.T], axis=0)
    shard = jnp.stack([shard[:, :hh], shard[:, hh:]])
    ids = cluster_ids.reshape(1, rows)
    params = functools.partial(
        pltpu.CompilerParams, has_side_effects=True, vmem_limit_bytes=50 * 2**20
    )
    w0, w1 = d // 2 + LAB, d // 2
    s0, s1 = pl.pallas_call(
        functools.partial(encode_kernel, n, nx),
        out_shape=[
            jax.ShapeDtypeStruct((2 * dp, w0), BF16),
            jax.ShapeDtypeStruct((2 * dp, w1), BF16),
        ],
        in_specs=[VM] * 7,
        out_specs=[VM] * 2,
        scratch_shapes=[
            pltpu.VMEM((2, 2, n, n, 16, hh), BF16),
            pltpu.VMEM((nx, toks, d), BF16),
            pltpu.VMEM((d, hid), BF16),
            pltpu.VMEM((d, hid), BF16),
            pltpu.VMEM((3, toks, d), BF16),
            pltpu.VMEM((2, toks // 2, d), BF16),
            pltpu.VMEM((2, toks, d), BF16),
            pltpu.VMEM((rows, d), BF16),
            DMA((2,)),
            DMA((2, n)),
            DMA((2, n)),
            DMA((2, 2, n)),
            DMA((2, 2, n)),
            DMA((2, n)),
            DMA((2, n)),
            DMA((4,)),
            DMA((4,)),
            DMA((2,)),
            DMA((2,)),
            DMA((6,)),
            DMA((6,)),
        ],
        compiler_params=params(collective_id=0),
    )(
        shard,
        tokens,
        b_up.reshape(1, hid),
        ln_gain.reshape(1, d),
        doc_lengths,
        pool_rows,
        ids,
    )
    nyc = 2 * n
    out = pl.pallas_call(
        functools.partial(search_kernel, n, nx),
        out_shape=jax.ShapeDtypeStruct((1, rows), F32),
        in_specs=[VM] * 3,
        out_specs=VM,
        scratch_shapes=[
            pltpu.VMEM((nyc, 2 * n, w0), BF16),
            pltpu.VMEM((n, 2 * nyc, w0), BF16),
            pltpu.VMEM((n, 2 * nyc, w0), BF16),
            pltpu.VMEM((n, 2 * nyc, w1), BF16),
            pltpu.VMEM((nyc, 2 * n, w1), BF16),
            pltpu.VMEM((nyc, 2 * n, w1), BF16),
            pltpu.VMEM((3, 2 * dp, w0 + w1), BF16),
            pltpu.VMEM((n, 2 * dp), F32),
            pltpu.VMEM((8, 2 * dp), F32),
            pltpu.VMEM((8, 2 * dp), F32),
            pltpu.VMEM((8, 2 * dp), F32),
            pltpu.VMEM((n, 1, 2 * dp), F32),
            pltpu.VMEM((nyc, n, 2 * dp), F32),
            DMA((6,)),
            DMA((nyc,)),
            DMA((nyc,)),
            DMA((n,)),
            DMA((n,)),
            DMA((n,)),
            DMA((n,)),
            DMA((nyc,)),
            DMA((nyc,)),
            DMA((2,)),
            DMA((2,)),
            DMA((1,)),
            DMA((1,)),
            DMA((n,)),
            DMA((n,)),
            DMA((nyc,)),
            DMA((nyc,)),
        ],
        compiler_params=params(collective_id=1),
    )(s0.reshape(nyc, 2 * n, w0), s1.reshape(n, 2 * nyc, w1), ids)
    return out.reshape(rows)


def solution(mesh):
    n = math.isqrt(mesh.shape["dp"] // 2)
    placed = (
        P(("dp", "split"), None),
        P("dp", "split"),
        P("split"),
        P("split", "dp"),
        P(),
        P(("dp", "split"), None),
        P(("dp", "split"), None),
        P(("dp", "split")),
    )
    return jax.shard_map(
        functools.partial(on_device, n, mesh.shape["split"]),
        mesh=mesh,
        in_specs=placed,
        out_specs=P(("dp", "split")),
        check_vma=False,
    )
```

time: 304 us -> 112 us (0.37)
  waiting for transfers between devices: 175 us -> 0 us
  Pallas kernels: 0 us -> 107 us
  blocking collectives: 68.1 us -> 0 us
  starting transfers between devices: 19.9 us -> 0 us
  between operations: 13.3 us -> 0.03 us
  matrix products: 11.1 us -> 0 us
  local copies, waits for them, and re-layouts: 10.1 us -> 3.78 us
  other arithmetic: 6.65 us -> 0.71 us
    all_gather x3 -> x0, waiting for transfers between devices: 152 us -> none  [the longest x1 84.6 us: expand(): down_full = lax.all_gather(down_part, 'dp', axis=1, tiled=True)]
    pallas_call x0 -> x2, Pallas kernels: none -> 107 us  [the longest x1 54.1 us: on_device(): pl.pallas_call(functools.partial(search_kernel, n, nx), out_shape=jax.Sha...]
    all_gather x4 -> x0, blocking collectives: 38.3 us -> none  [the longest x1 11.8 us: on_device(): lax.all_gather(w_up, 'split', axis=1, tiled=True)]
    all_to_all x1 -> x0, blocking collectives: 29.7 us -> none  [on_device(): lax.all_to_all(send_rows, 'dp', split_axis=0, concat_axis=0, tiled=True)]
    all_to_all x2 -> x0, waiting for transfers between devices: 22.8 us -> none  [the longest x1 11.4 us: on_device(): lax.all_to_all(best.reshape(owner_count, capacity), 'dp', split_axis=0, c...]
    all_to_all x2 -> x0, starting transfers between devices: 19.8 us -> none  [the longest x1 14.3 us: on_device(): lax.all_to_all(best.reshape(owner_count, capacity), 'dp', split_axis=0, c...]
    dot_general x3 -> x0, matrix products: 11.1 us -> none  [the longest x1 7.96 us: on_device(): ffn_out = jnp.dot(hidden, down_full, preferred_element_type=jnp.float32)]
    gather x4 -> x0, local copies, waits for them, and re-layouts: 5 us -> none  [the longest x1 1.87 us: on_device(): label[slot_row]]
  transfers between devices with their start and end apart: 5 -> 0, of which waited for: 5 -> 0; matrix products, arithmetic and copies ran while one was open for 3% -> 0% of each run, Pallas kernels for 0% -> 0%
where the time goes in v1:
time: 112 us; the launch traced here: 111 us
  Pallas kernels  107 us (96%)
  local copies, waits for them, and re-layouts  3.78 us (3%)
    pallas_call x1, Pallas kernels, on_device(): pl.pallas_call(functools.partial(search_kernel, n, nx), out_shape=jax.Sha...  54.1 us
    pallas_call x1, Pallas kernels, on_device(): pl.pallas_call(functools.partial(encode_kernel, n, nx), out_shape=[jax.Sh...  52.8 us
    unnamed x13, local copies, waits for them, and re-layouts  3.09 us

profile of v1, /device:TPU:1, one launch (start us, length us, event | category | flops | bytes accessed | tf_op | source)
XLA Modules:
  0.0 111.4 jit_solution(13572974311341661907)
XLA Ops:
  0.0 0.0 copy-start.5
  0.0 0.7 reshape.18.bias
  0.7 0.0 copy-done.5
  0.7 0.7 fusion.1
  1.4 0.0 copy-start.2
  1.4 0.0 copy-start.3
  1.4 0.0 copy-start.4
  1.4 0.7 copy-done.2
  2.1 0.0 copy-done.3
  2.1 0.0 copy-done.4
  2.1 0.0 copy-start
  2.1 0.9 copy-done
  3.1 0.0 copy-start.1
  3.1 0.9 copy-done.1
  4.0 52.8 %shard_map.82 = (bf16[256,640]{1,0:T(8,128)(2,1)S(1)}, bf16[256,512]{1,0:T(8,128)(2,1)S(1)}) custom-call(bf16[2,16,256]{2,1,0:T(8,128)(2,1)S(1)} %pad_maximum_fusion.shard, bf16[128,1024]{1,0:T(8,128)(2,1)S(1)} %copy-done, bf16[1,512]{1,0:T(2,128)(2,1)S(1)} %reshape.18.bias, f32[1,1024]{1,0:T(1,128)S(1)} %bitcast.12, s32[1,16]{1,0:T(1,128)S(1)} %copy-done.4, ...), custom_call_target="tpu_custom_call" | custom-call | tf_op jit(solution)/shard_map/pallas_call | solution.py:446
  56.8 54.1 %shard_map.83 = f32[1,128]{1,0:T(1,128)S(1)} custom-call(bf16[16,16,640]{2,1,0:T(8,128)(2,1)S(1)} %bitcast.10, bf16[8,32,512]{2,1,0:T(8,128)(2,1)S(1)} %bitcast.11, s32[1,128]{1,0:T(1,128)S(1)} %bitcast.14), custom_call_target="tpu_custom_call" | custom-call | tf_op jit(solution)/shard_map/pallas_call | solution.py:488
  110.9 0.5 copy.10
  (1 shorter events, 0.0 us)
Async XLA Ops:
  0.0 0.7 copy-start.5
  1.4 0.7 copy-start.2
  1.4 0.7 copy-start.3
  1.4 0.7 copy-start.4
  2.1 1.0 copy-start
  3.1 0.9 copy-start.1

commit v2 on v0

v2 whole, which is shorter than its diff:
```python
import functools
import math

import jax
import jax.numpy as jnp
from jax import lax
from jax.experimental import pallas as pl
from jax.experimental.pallas import tpu as pltpu
from jax.sharding import PartitionSpec as P

MESH = pl.DeviceIdType.MESH
F32, BF16 = jnp.float32, jnp.bfloat16
LAB = 128


def iota(shape, dim):
    return lax.broadcasted_iota(jnp.int32, shape, dim)


def mm(a, b):
    return jnp.dot(a, b, preferred_element_type=F32)


def mm_nt(a, b):
    return lax.dot_general(a, b, (((1,), (1,)), ((), ())), preferred_element_type=F32)


def unit_rows(v):
    return (v * lax.rsqrt(jnp.sum(v * v, axis=1, keepdims=True) + 1e-06)).astype(BF16)


def here(n):
    me = lax.axis_index("dp")
    return me, me // (2 * n), (me // 2) % n, me % 2, lax.axis_index("split")


def to_column(row, size):
    eye = iota((size, size), 0) == iota((size, size), 1)
    return jnp.sum(jnp.where(eye, row, 0.0), axis=1, keepdims=True)


def slots(ids_ref, n):
    dp = 2 * n * n
    rows = ids_ref.shape[1]
    ids = ids_ref[...]
    owner, label = ids & (dp - 1), ids >> int(math.log2(dp))
    owner_col = to_column(owner.astype(F32), rows)
    same = owner_col == owner.astype(F32)
    before = iota((rows, rows), 0) < iota((rows, rows), 1)
    place = jnp.sum(jnp.where(same & before, 1.0, 0.0), axis=0, keepdims=True).astype(jnp.int32)
    return owner, place, to_column(label.astype(F32), rows)


def remote(src, dst, send, recv, dev):
    return pltpu.make_async_remote_copy(
        src_ref=src, dst_ref=dst, send_sem=send, recv_sem=recv, device_id=dev, device_id_type=MESH
    )


def exchange(src, dst, mine, count, dev, send, recv, spread=False):
    def piece(other):
        return src if spread else src.at[other]

    def start():
        @pl.loop(1, count)
        def _(k):
            other = (mine + k) % count
            remote(piece(other), dst.at[mine], send.at[other], recv.at[mine], dev(other)).start()

        dst[mine] = src[...] if spread else src[mine]

    def wait():
        @pl.loop(1, count)
        def _(k):
            other = (mine + k) % count
            remote(piece(other), dst.at[other], send.at[other], recv.at[other], dev(other)).wait()

    return start, wait


def kernel(
    n, nx, tok_in, w_up, w_down, bias, gain, lengths, pool_in, ids, out,
    tok, pool, shard, G, T, up, down, PS, RA, emb,
    SL, RL, TL, L, SP, RP, TP, FP, SQ, RQ, TQ, FQ, E, B1, B2, BM, LR, B3,
    lsem, p1s, p1r, ws, wr, sibs, sibr, ts, tr, qs, qr,
    yls, ylr, zls, zlr, lxs, lxr, yps, ypr, zps, zpr, zqs, zqr, yqs, yqr, es, er,
    b1s, b1r, bms, bmr, b2s, b2r,
):
    me, z, y, c, x = here(n)
    nyc = 2 * n
    yc = me % nyc
    dp = nyc * n
    total = 2 * dp
    hh = shard.shape[2]
    toks, d = tok.shape
    rows = ids.shape[1]
    xp, xm, xo = (x + 1) % nx, (x + nx - 1) % nx, (x + 2) % nx

    def at_z(zz):
        return (zz * nyc + yc, x)

    def at_y(yy):
        return ((z * n + yy) * 2 + c, x)

    def at_yc(other):
        return (z * nyc + other, x)

    place = (y, z)
    ring = (at_y, at_z)
    first = (at_z, at_y)
    sibling = (me + 1 - 2 * c, x)

    load_tok = pltpu.make_async_copy(tok_in, tok, lsem.at[0])
    load_pool = pltpu.make_async_copy(pool_in, pool, lsem.at[1])
    load_tok.start()
    load_pool.start()

    barrier = pltpu.get_barrier_semaphore()

    def greet(dev):
        pl.semaphore_signal(barrier, 1, device_id=dev, device_id_type=MESH)

    @pl.loop(1, n)
    def _(k):
        zz = (z + k) % n
        greet(at_z(zz))
        greet((zz * nyc + yc, xp))

    @pl.loop(1, nyc)
    def _(k):
        greet(at_yc((yc + k) % nyc))

    for other in (xp, xm, xo):
        greet((me, other))

    both = jnp.concatenate([w_up[...].astype(F32), w_down[...].astype(F32)], axis=0).astype(BF16)
    shard[0] = both[:, :hh]
    shard[1] = both[:, hh:]
    load_tok.wait()
    pl.semaphore_wait(barrier, 2 * (n - 1) + nyc - 1 + 3)

    def first_hop(h, k):
        mine = (z, y)[h]
        other = (mine + k) % n
        slot = G.at[c, 0, y, z] if h == 0 else G.at[c, 1, z, y]
        return remote(shard.at[h], slot, p1s.at[h, other], p1r.at[h, mine], first[h](other))

    @pl.loop(1, n)
    def _(k):
        first_hop(0, k).start()
        first_hop(1, k).start()

    t_send = [
        remote(tok, T.at[0], ts.at[0], tr.at[0], (me, xp)),
        remote(tok, T.at[1], ts.at[1], tr.at[1], (me, xm)),
        remote(tok, T.at[2], ts.at[2], tr.at[2], (me, xo)),
    ]
    for t in t_send:
        t.start()
    G[c, 0, y, z] = shard[0]
    G[c, 1, z, y] = shard[1]

    owner, place_in, label_col = slots(ids, n)
    slot = iota((total, rows), 0)
    target0 = ((owner % nyc) * n + owner // nyc) * 2 + place_in
    target1 = owner * 2 + place_in
    pick0 = jnp.where(slot == target0, 1.0, 0.0).astype(BF16)
    pick1 = jnp.where(slot == target1, 1.0, 0.0).astype(BF16)
    lab = jnp.broadcast_to(label_col + 1.0, (rows, LAB)).astype(BF16)
    SL[...] = mm(pick0, lab).astype(BF16).reshape(nyc, 2 * n, LAB)
    lab_y = exchange(SL, RL, yc, nyc, at_yc, yls, ylr)
    lab_z = exchange(TL, L.at[0], z, n, at_z, zls, zlr)
    lab_y[0]()

    @pl.loop(1, n)
    def _(k):
        for h in range(2):
            mine = (z, y)[h]
            other = (mine + k) % n
            slot_ = G.at[c, 0, y, other] if h == 0 else G.at[c, 1, z, other]
            remote(shard.at[h], slot_, p1s.at[h, other], p1r.at[h, other], first[h](other)).wait_recv()

    def second_hop(h, k):
        q = place[h]
        other = (q + k) % n
        return remote(G.at[c, h, q], G.at[c, h, q], ws.at[h, other], wr.at[h, q], ring[h](other))

    def to_sibling(h, i):
        return remote(G.at[c, h, i], G.at[c, h, i], sibs.at[h, i], sibr.at[h, i], sibling)

    @pl.loop(1, n)
    def _(k):
        second_hop(0, k).start()
        second_hop(1, k).start()

    to_sibling(0, y).start()
    to_sibling(1, z).start()

    load_pool.wait()
    pool_n = pool.shape[0]
    emb[0:pool_n, :] = unit_rows(pool[...].astype(F32))

    row, col = iota((total, total), 0), iota((total, total), 1)
    z_, yc_, s_ = row // (2 * nyc), (row // 2) % nyc, row % 2
    by_z = jnp.where(col == (yc_ * n + z_) * 2 + s_, 1.0, 0.0).astype(BF16)
    yc_, z_ = row // (2 * n), (row // 2) % n
    by_yc = jnp.where(col == (z_ * nyc + yc_) * 2 + s_, 1.0, 0.0).astype(BF16)
    eye = row == col
    lab_y[1]()
    TL[...] = mm(by_z, RL[...].reshape(total, LAB)).astype(BF16).reshape(n, 2 * nyc, LAB)
    lab_z[0]()

    @pl.loop(1, n)
    def _(k):
        for h in range(2):
            other = (place[h] + k) % n
            g = G.at[c, h, other]
            remote(g, g, ws.at[h, other], wr.at[h, other], ring[h](other)).wait_recv()
            to_sibling(h, other).start()

    lab_z[1]()
    lx = [
        remote(L.at[0], L.at[1], lxs.at[0], lxr.at[0], (me, xp)),
        remote(L.at[0], L.at[2], lxs.at[1], lxr.at[1], (me, xm)),
    ]
    for t in lx:
        t.start()

    m = n * 16
    o, i_ = iota((2 * m, 2 * m), 0), iota((2 * m, 2 * m), 1)
    w_, rest = o // m, o % m
    n_, c_, r_ = rest // 16, (rest // 8) % 2, rest % 8
    order = jnp.where(i_ == c_ * m + n_ * 16 + w_ * 8 + r_, 1.0, 0.0).astype(BF16)

    @pl.loop(0, n)
    def _(i):
        for h in range(2):
            g = G.at[1 - c, h, i]
            remote(g, g, sibs.at[h, i], sibr.at[h, i], sibling).wait_recv()

    @pl.loop(0, n)
    def _(i):
        for h in range(2):
            pair = jnp.concatenate([G[0, h, i].reshape(m, hh), G[1, h, i].reshape(m, hh)], axis=0)
            w = mm(order, pair).astype(BF16)
            cols = slice(h * hh, (h + 1) * hh)
            for ref, part in ((up, w[:m]), (down, w[m:])):
                if h == 0:
                    for zz in range(n):
                        at = pl.multiple_of((zz * n + i) * 16, 16)
                        ref[pl.ds(at, 16), cols] = part[zz * 16 : (zz + 1) * 16]
                else:
                    ref[pl.ds(pl.multiple_of(i * m, m), m), cols] = part

    def ffn(block):
        pre = mm(block, up[...]) + bias[...].astype(F32)
        hidden = (0.5 * pre * (1.0 + lax.erf(pre * (0.5**0.5)))).astype(BF16)
        return mm_nt(hidden, down[...])

    sums = []
    for j, (held, to) in enumerate(((2, xo), (1, xp), (0, xm))):
        t_send[held].wait_recv()
        PS[j] = ffn(T[held]).astype(BF16)
        sums.append(remote(PS.at[j], RA.at[j], qs.at[j], qr.at[j], (me, to)))
        sums[-1].start()
    state = tok[...].astype(F32) + ffn(tok[...])
    for q in sums:
        q.wait_recv()
    for j in range(3):
        state = state + RA[j].astype(F32)

    mean = jnp.mean(state, axis=1, keepdims=True)
    centred = state - mean
    var = jnp.mean(centred * centred, axis=1, keepdims=True)
    normed = centred * lax.rsqrt(var + 1e-05) * gain[...]
    docs = lengths.shape[1]
    len_row = lengths[...].astype(F32)
    len_col = to_column(len_row, docs)
    upto = iota((docs, docs), 1) <= iota((docs, docs), 0)
    ends = jnp.sum(jnp.where(upto, len_row, 0.0), axis=1, keepdims=True)
    places = iota((docs, toks), 1).astype(F32)
    member = jnp.where((places >= ends - len_col) & (places < ends), 1.0, 0.0)
    pooled = (
        jnp.dot(member, normed, precision=lax.Precision.HIGHEST, preferred_element_type=F32)
        / len_col
    )
    emb[pool_n : pool_n + docs, :] = unit_rows(pooled)

    w = d // 4
    p_y = [exchange(SP.at[k], RP.at[k], yc, nyc, at_yc, yps.at[k], ypr.at[k]) for k in range(2)]
    p_z = [exchange(TP.at[k], FP.at[k], z, n, at_z, zps.at[k], zpr.at[k]) for k in range(2)]
    q_z = [exchange(SQ.at[k], RQ.at[k], z, n, at_z, zqs.at[k], zqr.at[k]) for k in range(2)]
    q_y = [exchange(TQ.at[k], FQ.at[k], yc, nyc, at_yc, yqs.at[k], yqr.at[k]) for k in range(2)]
    for k in range(2):
        e0 = emb[:, 2 * k * w : (2 * k + 1) * w]
        e1 = emb[:, (2 * k + 1) * w : (2 * k + 2) * w]
        SP[k] = mm(pick0, e0).astype(BF16).reshape(nyc, 2 * n, w)
        p_y[k][0]()
        SQ[k] = mm(pick1, e1).astype(BF16).reshape(n, 2 * nyc, w)
        q_z[k][0]()
    for k in range(2):
        p_y[k][1]()
        TP[k] = mm(by_z, RP[k].reshape(total, w)).astype(BF16).reshape(n, 2 * nyc, w)
        p_z[k][0]()
        q_z[k][1]()
        TQ[k] = mm(by_yc, RQ[k].reshape(total, w)).astype(BF16).reshape(nyc, 2 * n, w)
        q_y[k][0]()

    xs = []
    for k in range(2):
        p_z[k][1]()
        E[0, k, :, :w] = FP[k].reshape(total, w)
        q_y[k][1]()
        E[0, k, :, w:] = mm(by_z, FQ[k].reshape(total, w)).astype(BF16)
        xs.append(remote(E.at[0, k], E.at[1, k], es.at[0, k], er.at[0, k], (me, xp)))
        xs.append(remote(E.at[0, k], E.at[2, k], es.at[1, k], er.at[1, k], (me, xm)))
        xs[-2].start()
        xs[-1].start()

    for t in lx:
        t.wait_recv()

    def labels(i):
        column = L[i].reshape(total, LAB)[:, 0:1].astype(F32)
        return column, jnp.sum(jnp.where(eye, column, 0.0), axis=0, keepdims=True)

    (col0, row0), (col1, row1), (col2, _) = labels(0), labels(1), labels(2)

    def part(j, i, k):
        return mm_nt(E[j, k], E[i, k])

    def best_of(sc, keep):
        return jnp.max(jnp.where(keep, sc, -1.0), axis=0, keepdims=True)

    best = best_of(part(0, 0, 0) + part(0, 0, 1), (col0 == row0) & ~eye)
    xs[0].wait_recv()
    xs[1].wait_recv()
    s21, s10, s20 = part(2, 1, 0), part(1, 0, 0), part(2, 0, 0)
    xs[2].wait_recv()
    xs[3].wait_recv()
    B1[1] = jnp.broadcast_to(best_of(s21 + part(2, 1, 1), col2 == row1), B1.shape[1:])
    over = B1.at[1, pl.ds(0, 1)]

    @pl.loop(0, n)
    def _(zz):
        remote(over, BM.at[z], bms.at[zz], bmr.at[z], (zz * nyc + yc, xm)).start()

    best = jnp.maximum(best, best_of(s10 + part(1, 0, 1), col1 == row0))
    best = jnp.maximum(best, best_of(s20 + part(2, 0, 1), col2 == row0))
    B1[0] = jnp.broadcast_to(best, B1.shape[1:])

    back_z = exchange(B1.at[0, pl.ds(0, 1)], B2, z, n, at_z, b1s, b1r, spread=True)
    back_z[0]()

    @pl.loop(0, n)
    def _(zz):
        remote(over, BM.at[zz], bms.at[zz], bmr.at[zz], (zz * nyc + yc, xm)).wait()

    back_z[1]()
    both_ = jnp.maximum(B2[...], BM[...]).reshape(n, total)
    LR[...] = pltpu.roll(both_, (total - z * 2 * nyc) % total, 1)[:, : LR.shape[1]]
    back_y = exchange(LR, B3, yc, nyc, at_yc, b2s, b2r, spread=True)
    back_y[0]()
    back_y[1]()
    got = B3[...].reshape(dp, LR.shape[1])
    lane = iota(got.shape, 1)
    v0 = jnp.sum(jnp.where(lane == yc * 2, got, 0.0), axis=1, keepdims=True)
    v1 = jnp.sum(jnp.where(lane == yc * 2 + 1, got, 0.0), axis=1, keepdims=True)
    mine = iota((dp, rows), 0) == (owner % nyc) * n + owner // nyc
    out[...] = jnp.sum(jnp.where(mine, jnp.where(place_in == 0, v0, v1), 0.0), axis=0, keepdims=True)

    @pl.loop(1, n)
    def _(k):
        for h in range(2):
            first_hop(h, k).wait_send()
            second_hop(h, k).wait_send()

    @pl.loop(0, n)
    def _(i):
        to_sibling(0, i).wait_send()
        to_sibling(1, i).wait_send()

    for t in [*t_send, *sums, *lx, *xs]:
        t.wait_send()


VM = pl.BlockSpec(memory_space=pltpu.VMEM)
ANY = pl.BlockSpec(memory_space=pl.ANY)


def on_device(n, nx, tokens, w_up, b_up, w_down, ln_gain, doc_lengths, pool_rows, cluster_ids):
    toks, d = tokens.shape
    hid = w_up.shape[1]
    hh = hid // 2
    rows = cluster_ids.shape[0]
    nyc = 2 * n
    dp = nyc * n
    total = 2 * dp
    w = d // 4
    keep = min(total, 128)

    def vm(*shape):
        return pltpu.VMEM(shape, BF16)

    def vf(*shape):
        return pltpu.VMEM(shape, F32)

    def two(*shape):
        return [pltpu.SemaphoreType.DMA(shape)] * 2

    out = pl.pallas_call(
        functools.partial(kernel, n, nx),
        out_shape=jax.ShapeDtypeStruct((1, rows), F32),
        in_specs=[ANY, VM, VM, VM, VM, VM, ANY, VM],
        out_specs=VM,
        scratch_shapes=[
            vm(toks, d),
            vm(*pool_rows.shape),
            vm(2, 16, hh),
            vm(2, 2, n, n, 16, hh),
            vm(3, toks, d),
            vm(d, hid),
            vm(d, hid),
            vm(3, toks, d),
            vm(3, toks, d),
            vm(rows, d),
            vm(nyc, 2 * n, LAB),
            vm(nyc, 2 * n, LAB),
            vm(n, 2 * nyc, LAB),
            vm(3, n, 2 * nyc, LAB),
            vm(2, nyc, 2 * n, w),
            vm(2, nyc, 2 * n, w),
            vm(2, n, 2 * nyc, w),
            vm(2, n, 2 * nyc, w),
            vm(2, n, 2 * nyc, w),
            vm(2, n, 2 * nyc, w),
            vm(2, nyc, 2 * n, w),
            vm(2, nyc, 2 * n, w),
            vm(3, 2, total, 2 * w),
            vf(2, 8, total),
            vf(n, 1, total),
            vf(n, 1, total),
            vf(n, keep),
            vf(nyc, n, keep),
            pltpu.SemaphoreType.DMA((2,)),
            *two(2, n),
            *two(2, n),
            *two(2, n),
            *two(3),
            *two(3),
            *two(nyc),
            *two(n),
            *two(2),
            *two(2, nyc),
            *two(2, n),
            *two(2, n),
            *two(2, nyc),
            *two(2, 2),
            *two(n),
            *two(n),
            *two(nyc),
        ],
        compiler_params=pltpu.CompilerParams(
            collective_id=0, has_side_effects=True, vmem_limit_bytes=58 * 2**20
        ),
    )(
        tokens,
        w_up,
        w_down.T,
        b_up.reshape(1, hid),
        ln_gain.reshape(1, d),
        doc_lengths,
        pool_rows,
        cluster_ids.reshape(1, rows),
    )
    return out.reshape(rows)


def solution(mesh):
    n = math.isqrt(mesh.shape["dp"] // 2)
    placed = (
        P(("dp", "split"), None),
        P("dp", "split"),
        P("split"),
        P("split", "dp"),
        P(),
        P(("dp", "split"), None),
        P(("dp", "split"), None),
        P(("dp", "split")),
    )
    return jax.shard_map(
        functools.partial(on_device, n, mesh.shape["split"]),
        mesh=mesh,
        in_specs=placed,
        out_specs=P(("dp", "split")),
        check_vma=False,
    )
```

time: 304 us -> 101 us (0.33)
  waiting for transfers between devices: 175 us -> 0 us
  Pallas kernels: 0 us -> 98.7 us
  blocking collectives: 68.1 us -> 0 us
  starting transfers between devices: 19.9 us -> 0 us
  between operations: 13.3 us -> 0.02 us
  matrix products: 11.1 us -> 0 us
  local copies, waits for them, and re-layouts: 10.1 us -> 2.41 us
  other arithmetic: 6.65 us -> 0 us
    all_gather x3 -> x0, waiting for transfers between devices: 152 us -> none  [the longest x1 84.6 us: expand(): down_full = lax.all_gather(down_part, 'dp', axis=1, tiled=True)]
    pallas_call x0 -> x1, Pallas kernels: none -> 98.7 us  [on_device(): pl.pallas_call(functools.partial(kernel, n, nx), out_shape=jax.ShapeDtype...]
    all_gather x4 -> x0, blocking collectives: 38.3 us -> none  [the longest x1 11.8 us: on_device(): lax.all_gather(w_up, 'split', axis=1, tiled=True)]
    all_to_all x1 -> x0, blocking collectives: 29.7 us -> none  [on_device(): lax.all_to_all(send_rows, 'dp', split_axis=0, concat_axis=0, tiled=True)]
    all_to_all x2 -> x0, waiting for transfers between devices: 22.8 us -> none  [the longest x1 11.4 us: on_device(): lax.all_to_all(best.reshape(owner_count, capacity), 'dp', split_axis=0, c...]
    all_to_all x2 -> x0, starting transfers between devices: 19.8 us -> none  [the longest x1 14.3 us: on_device(): lax.all_to_all(best.reshape(owner_count, capacity), 'dp', split_axis=0, c...]
    dot_general x3 -> x0, matrix products: 11.1 us -> none  [the longest x1 7.96 us: on_device(): ffn_out = jnp.dot(hidden, down_full, preferred_element_type=jnp.float32)]
    gather x4 -> x0, local copies, waits for them, and re-layouts: 5 us -> none  [the longest x1 1.87 us: on_device(): label[slot_row]]
  transfers between devices with their start and end apart: 5 -> 0, of which waited for: 5 -> 0; matrix products, arithmetic and copies ran while one was open for 3% -> 0% of each run, Pallas kernels for 0% -> 0%
where the time goes in v2:
time: 101 us
  Pallas kernels  98.7 us (98%)
  local copies, waits for them, and re-layouts  2.41 us (2%)
    pallas_call x1, Pallas kernels, on_device(): pl.pallas_call(functools.partial(kernel, n, nx), out_shape=jax.ShapeDtype...  98.7 us

profile of v2, /device:TPU:1, one launch (start us, length us, event | category | flops | bytes accessed | tf_op | source)
XLA Modules:
  0.0 101.1 jit_solution(5608345596633091171)
XLA Ops:
  0.0 0.0 copy-start
  0.0 0.7 copy-done
  0.7 0.6 reshape.12.bias
  1.2 98.7 %shard_map.82 = f32[1,128]{1,0:T(1,128)} custom-call(bf16[128,1024]{1,0:T(8,128)(2,1)} %tok_in.1, bf16[8,512]{1,0:T(8,128)(2,1)} %w_up.1, bf16[8,512]{1,0:T(8,128)(2,1)} %bitcast.4, bf16[1,512]{1,0:T(2,128)(2,1)} %reshape.12.bias, f32[1,1024]{1,0:T(1,128)} %bitcast.5, s32[1,16]{1,0:T(1,128)} %lengths.1, bf16[112,1024]{1,0:T(8,128)(2,1)} %pool_in.1, ...), custom_call_target="tpu_custom_call" | custom-call | tf_op jit(solution)/shard_map/pallas_call | solution.py:411
  100.0 0.0 copy-start.1
  100.0 0.7 copy-done.1
  100.6 0.5 copy.10
Async XLA Ops:
  0.0 0.7 copy-start
  100.0 0.7 copy-start.1

commit v3 on v2

--- a/solution.py
+++ b/solution.py
@@ -79,8 +79,8 @@
 
 
 def kernel(
-    n, nx, tok_in, w_up, w_down, bias, gain, lengths, pool_in, ids, out,
-    tok, pool, shard, G, T, up, down, PS, RA, emb,
+    n, nx, tok_in, w_up_in, w_down_in, bias_in, gain_in, lengths_in, pool_in, ids_in, out,
+    tok, w_up, w_down, bias, gain, lengths, pool, ids, shard, G, T, up, down, PS, RA, RF, emb,
     SL, RL, TL, L, SP, RP, TP, FP, SQ, RQ, TQ, FQ, E, B1, B2, BM, LR, B3,
     lsem, p1s, p1r, ws, wr, sibs, sibr, ts, tr, qs, qr,
     yls, ylr, zls, zlr, lxs, lxr, yps, ypr, zps, zpr, zqs, zqr, yqs, yqr, es, er,
@@ -110,34 +110,43 @@
     first = (at_z, at_y)
     sibling = (me + 1 - 2 * c, x)
 
-    load_tok = pltpu.make_async_copy(tok_in, tok, lsem.at[0])
-    load_pool = pltpu.make_async_copy(pool_in, pool, lsem.at[1])
-    load_tok.start()
-    load_pool.start()
-
     barrier = pltpu.get_barrier_semaphore()
 
     def greet(dev):
         pl.semaphore_signal(barrier, 1, device_id=dev, device_id_type=MESH)
 
+    for other in (xp, xm, xo):
+        greet((me, other))
+    greet(sibling)
+
     @pl.loop(1, n)
     def _(k):
-        zz = (z + k) % n
-        greet(at_z(zz))
-        greet((zz * nyc + yc, xp))
-
-    @pl.loop(1, nyc)
-    def _(k):
-        greet(at_yc((yc + k) % nyc))
-
-    for other in (xp, xm, xo):
-        greet((me, other))
-
+        greet(at_z((z + k) % n))
+        greet(at_y((y + k) % n))
+
+    loads = [
+        pltpu.make_async_copy(src, dst, lsem.at[k])
+        for k, (src, dst) in enumerate(
+            (
+                (w_up_in, w_up),
+                (w_down_in, w_down),
+                (tok_in, tok),
+                (ids_in, ids),
+                (pool_in, pool),
+                (bias_in, bias),
+                (gain_in, gain),
+                (lengths_in, lengths),
+            )
+        )
+    ]
+    for load in loads:
+        load.start()
+    for load in loads[:3]:
+        load.wait()
     both = jnp.concatenate([w_up[...].astype(F32), w_down[...].astype(F32)], axis=0).astype(BF16)
     shard[0] = both[:, :hh]
     shard[1] = both[:, hh:]
-    load_tok.wait()
-    pl.semaphore_wait(barrier, 2 * (n - 1) + nyc - 1 + 3)
+    pl.semaphore_wait(barrier, 2 * (n - 1) + 4)
 
     def first_hop(h, k):
         mine = (z, y)[h]
@@ -160,6 +169,7 @@
     G[c, 0, y, z] = shard[0]
     G[c, 1, z, y] = shard[1]
 
+    loads[3].wait()
     owner, place_in, label_col = slots(ids, n)
     slot = iota((total, rows), 0)
     target0 = ((owner % nyc) * n + owner // nyc) * 2 + place_in
@@ -170,7 +180,6 @@
     SL[...] = mm(pick0, lab).astype(BF16).reshape(nyc, 2 * n, LAB)
     lab_y = exchange(SL, RL, yc, nyc, at_yc, yls, ylr)
     lab_z = exchange(TL, L.at[0], z, n, at_z, zls, zlr)
-    lab_y[0]()
 
     @pl.loop(1, n)
     def _(k):
@@ -193,10 +202,12 @@
         second_hop(0, k).start()
         second_hop(1, k).start()
 
+    lab_y[0]()
     to_sibling(0, y).start()
     to_sibling(1, z).start()
 
-    load_pool.wait()
+    for load in loads[4:]:
+        load.wait()
     pool_n = pool.shape[0]
     emb[0:pool_n, :] = unit_rows(pool[...].astype(F32))
 
@@ -253,21 +264,41 @@
                     ref[pl.ds(pl.multiple_of(i * m, m), m), cols] = part
 
     def ffn(block):
-        pre = mm(block, up[...]) + bias[...].astype(F32)
+        pre = mm(block, up[...]) + bias[...].astype(F32).reshape(1, up.shape[1])
         hidden = (0.5 * pre * (1.0 + lax.erf(pre * (0.5**0.5)))).astype(BF16)
         return mm_nt(hidden, down[...])
 
+    half = toks // 2
+    lo, hi = pl.ds(0, half), pl.ds(half, half)
     sums = []
-    for j, (held, to) in enumerate(((2, xo), (1, xp), (0, xm))):
-        t_send[held].wait_recv()
-        PS[j] = ffn(T[held]).astype(BF16)
-        sums.append(remote(PS.at[j], RA.at[j], qs.at[j], qr.at[j], (me, to)))
+
+    def give(j, rows_, dst, to):
+        k = len(sums)
+        sums.append(remote(PS.at[j, rows_], dst, qs.at[k], qr.at[k], (me, to)))
         sums[-1].start()
+
+    t_send[2].wait_recv()
+    PS[2] = ffn(T[2]).astype(BF16)
+    give(2, lo, RF.at[0], xp)
+    give(2, hi, RF.at[1], xm)
+    t_send[1].wait_recv()
+    right = ffn(T[1])
+    PS[1, hi] = right[half:].astype(BF16)
+    give(1, hi, RA.at[0, hi], xp)
+    t_send[0].wait_recv()
+    left = ffn(T[0])
+    PS[0, lo] = left[:half].astype(BF16)
+    give(0, lo, RA.at[1, lo], xm)
+    sums[0].wait_recv()
+    PS[1, lo] = (right[:half] + RF[0].astype(F32)).astype(BF16)
+    give(1, lo, RA.at[0, lo], xp)
+    sums[1].wait_recv()
+    PS[0, hi] = (left[half:] + RF[1].astype(F32)).astype(BF16)
+    give(0, hi, RA.at[1, hi], xm)
     state = tok[...].astype(F32) + ffn(tok[...])
-    for q in sums:
+    for q in sums[2:]:
         q.wait_recv()
-    for j in range(3):
-        state = state + RA[j].astype(F32)
+    state = state + RA[0].astype(F32) + RA[1].astype(F32)
 
     mean = jnp.mean(state, axis=1, keepdims=True)
     centred = state - mean
@@ -384,7 +415,6 @@
         t.wait_send()
 
 
-VM = pl.BlockSpec(memory_space=pltpu.VMEM)
 ANY = pl.BlockSpec(memory_space=pl.ANY)
 
 
@@ -411,18 +441,25 @@
     out = pl.pallas_call(
         functools.partial(kernel, n, nx),
         out_shape=jax.ShapeDtypeStruct((1, rows), F32),
-        in_specs=[ANY, VM, VM, VM, VM, VM, ANY, VM],
-        out_specs=VM,
+        in_specs=[ANY] * 8,
+        out_specs=pl.BlockSpec(memory_space=pltpu.VMEM),
         scratch_shapes=[
             vm(toks, d),
+            vm(*w_up.shape),
+            vm(*w_up.shape),
+            vm(hid),
+            vf(1, d),
+            pltpu.VMEM(doc_lengths.shape, jnp.int32),
             vm(*pool_rows.shape),
+            pltpu.VMEM((1, rows), jnp.int32),
             vm(2, 16, hh),
             vm(2, 2, n, n, 16, hh),
             vm(3, toks, d),
             vm(d, hid),
             vm(d, hid),
             vm(3, toks, d),
-            vm(3, toks, d),
+            vm(2, toks, d),
+            vm(2, toks // 2, d),
             vm(rows, d),
             vm(nyc, 2 * n, LAB),
             vm(nyc, 2 * n, LAB),
@@ -442,12 +479,12 @@
             vf(n, 1, total),
             vf(n, keep),
             vf(nyc, n, keep),
-            pltpu.SemaphoreType.DMA((2,)),
+            pltpu.SemaphoreType.DMA((8,)),
             *two(2, n),
             *two(2, n),
             *two(2, n),
             *two(3),
-            *two(3),
+            *two(6),
             *two(nyc),
             *two(n),
             *two(2),
@@ -467,7 +504,7 @@
         tokens,
         w_up,
         w_down.T,
-        b_up.reshape(1, hid),
+        b_up,
         ln_gain.reshape(1, d),
         doc_lengths,
         pool_rows,

time: 101 us -> 99.7 us (0.987)
  local copies, waits for them, and re-layouts: 2.41 us -> 1.1 us
where the time goes in v3:
time: 99.7 us; the launch traced here: 99.5 us
  Pallas kernels  98.4 us (99%)
  local copies, waits for them, and re-layouts  1.1 us (1%)
    pallas_call x1, Pallas kernels, on_device(): pl.pallas_call(functools.partial(kernel, n, nx), out_shape=jax.ShapeDtype...  98.4 us

profile of v3, /device:TPU:1, one launch (start us, length us, event | category | flops | bytes accessed | tf_op | source)
XLA Modules:
  0.0 99.5 jit_solution(9233649993194675206)
XLA Ops:
  0.0 98.4 %shard_map.82 = f32[1,128]{1,0:T(1,128)} custom-call(bf16[128,1024]{1,0:T(8,128)(2,1)} %tok_in.1, bf16[8,512]{1,0:T(8,128)(2,1)} %w_up_in.1, bf16[8,512]{1,0:T(8,128)(2,1)} %bitcast.4, bf16[512]{0:T(512)(128)(2,1)} %bias_in.1, f32[1,1024]{1,0:T(1,128)} %bitcast.5, s32[1,16]{1,0:T(1,128)} %lengths_in.1, bf16[112,1024]{1,0:T(8,128)(2,1)} %pool_in.1, ...), custom_call_target="tpu_custom_call" | custom-call | tf_op jit(solution)/shard_map/pallas_call | solution.py:441
  98.4 0.0 copy-start
  98.4 0.6 copy-done
  99.0 0.5 copy.10
Async XLA Ops:
  98.4 0.6 copy-start

commit v4 on v3

--- a/solution.py
+++ b/solution.py
@@ -17,6 +17,14 @@
     return lax.broadcasted_iota(jnp.int32, shape, dim)
 
 
+def div(a, k):
+    return a >> (k.bit_length() - 1)
+
+
+def mod(a, k):
+    return a & (k - 1)
+
+
 def mm(a, b):
     return jnp.dot(a, b, preferred_element_type=F32)
 
@@ -43,7 +51,7 @@
     dp = 2 * n * n
     rows = ids_ref.shape[1]
     ids = ids_ref[...]
-    owner, label = ids & (dp - 1), ids >> int(math.log2(dp))
+    owner, label = mod(ids, dp), div(ids, dp)
     owner_col = to_column(owner.astype(F32), rows)
     same = owner_col == owner.astype(F32)
     before = iota((rows, rows), 0) < iota((rows, rows), 1)
@@ -172,7 +180,8 @@
     loads[3].wait()
     owner, place_in, label_col = slots(ids, n)
     slot = iota((total, rows), 0)
-    target0 = ((owner % nyc) * n + owner // nyc) * 2 + place_in
+    owner_at = mod(owner, nyc) * n + div(owner, nyc)
+    target0 = owner_at * 2 + place_in
     target1 = owner * 2 + place_in
     pick0 = jnp.where(slot == target0, 1.0, 0.0).astype(BF16)
     pick1 = jnp.where(slot == target1, 1.0, 0.0).astype(BF16)
@@ -181,6 +190,20 @@
     lab_y = exchange(SL, RL, yc, nyc, at_yc, yls, ylr)
     lab_z = exchange(TL, L.at[0], z, n, at_z, zls, zlr)
 
+    row, col = iota((total, total), 0), iota((total, total), 1)
+    eye = row == col
+    s_ = mod(row, 2)
+    from_ = (mod(div(row, 2), nyc) * n + div(row, 2 * nyc)) * 2 + s_
+    by_z = jnp.where(col == from_, 1.0, 0.0).astype(BF16)
+    from_ = (mod(div(row, 2), n) * nyc + div(row, 2 * n)) * 2 + s_
+    by_yc = jnp.where(col == from_, 1.0, 0.0).astype(BF16)
+
+    m = n * 16
+    o, i_ = iota((2 * m, 2 * m), 0), iota((2 * m, 2 * m), 1)
+    rest = mod(o, m)
+    from_ = mod(div(rest, 8), 2) * m + div(rest, 16) * 16 + div(o, m) * 8 + mod(rest, 8)
+    order = jnp.where(i_ == from_, 1.0, 0.0).astype(BF16)
+
     @pl.loop(1, n)
     def _(k):
         for h in range(2):
@@ -211,37 +234,20 @@
     pool_n = pool.shape[0]
     emb[0:pool_n, :] = unit_rows(pool[...].astype(F32))
 
-    row, col = iota((total, total), 0), iota((total, total), 1)
-    z_, yc_, s_ = row // (2 * nyc), (row // 2) % nyc, row % 2
-    by_z = jnp.where(col == (yc_ * n + z_) * 2 + s_, 1.0, 0.0).astype(BF16)
-    yc_, z_ = row // (2 * n), (row // 2) % n
-    by_yc = jnp.where(col == (z_ * nyc + yc_) * 2 + s_, 1.0, 0.0).astype(BF16)
-    eye = row == col
-    lab_y[1]()
-    TL[...] = mm(by_z, RL[...].reshape(total, LAB)).astype(BF16).reshape(n, 2 * nyc, LAB)
-    lab_z[0]()
-
-    @pl.loop(1, n)
+
+    def pass_on(h, other):
+        g = G.at[c, h, other]
+        remote(g, g, ws.at[h, other], wr.at[h, other], ring[h](other)).wait_recv()
+        to_sibling(h, other).start()
+
+    @pl.loop(1, n // 2)
     def _(k):
         for h in range(2):
-            other = (place[h] + k) % n
-            g = G.at[c, h, other]
-            remote(g, g, ws.at[h, other], wr.at[h, other], ring[h](other)).wait_recv()
-            to_sibling(h, other).start()
-
-    lab_z[1]()
-    lx = [
-        remote(L.at[0], L.at[1], lxs.at[0], lxr.at[0], (me, xp)),
-        remote(L.at[0], L.at[2], lxs.at[1], lxr.at[1], (me, xm)),
-    ]
-    for t in lx:
-        t.start()
-
-    m = n * 16
-    o, i_ = iota((2 * m, 2 * m), 0), iota((2 * m, 2 * m), 1)
-    w_, rest = o // m, o % m
-    n_, c_, r_ = rest // 16, (rest // 8) % 2, rest % 8
-    order = jnp.where(i_ == c_ * m + n_ * 16 + w_ * 8 + r_, 1.0, 0.0).astype(BF16)
+            pass_on(h, (place[h] + k) % n)
+            pass_on(h, (place[h] + n - k) % n)
+
+    for h in range(2):
+        pass_on(h, (place[h] + n // 2) % n)
 
     @pl.loop(0, n)
     def _(i):
@@ -289,6 +295,10 @@
     left = ffn(T[0])
     PS[0, lo] = left[:half].astype(BF16)
     give(0, lo, RA.at[1, lo], xm)
+    lab_y[1]()
+    TL[...] = mm(by_z, RL[...].reshape(total, LAB)).astype(BF16).reshape(n, 2 * nyc, LAB)
+    lab_z[0]()
+
     sums[0].wait_recv()
     PS[1, lo] = (right[:half] + RF[0].astype(F32)).astype(BF16)
     give(1, lo, RA.at[0, lo], xp)
@@ -329,6 +339,13 @@
         p_y[k][0]()
         SQ[k] = mm(pick1, e1).astype(BF16).reshape(n, 2 * nyc, w)
         q_z[k][0]()
+    lab_z[1]()
+    lx = [
+        remote(L.at[0], L.at[1], lxs.at[0], lxr.at[0], (me, xp)),
+        remote(L.at[0], L.at[2], lxs.at[1], lxr.at[1], (me, xm)),
+    ]
+    for t in lx:
+        t.start()
     for k in range(2):
         p_y[k][1]()
         TP[k] = mm(by_z, RP[k].reshape(total, w)).astype(BF16).reshape(n, 2 * nyc, w)
@@ -397,7 +414,7 @@
     lane = iota(got.shape, 1)
     v0 = jnp.sum(jnp.where(lane == yc * 2, got, 0.0), axis=1, keepdims=True)
     v1 = jnp.sum(jnp.where(lane == yc * 2 + 1, got, 0.0), axis=1, keepdims=True)
-    mine = iota((dp, rows), 0) == (owner % nyc) * n + owner // nyc
+    mine = iota((dp, rows), 0) == owner_at
     out[...] = jnp.sum(jnp.where(mine, jnp.where(place_in == 0, v0, v1), 0.0), axis=0, keepdims=True)
 
     @pl.loop(1, n)

time: 99.7 us -> 95.4 us (0.957)
  Pallas kernels: 98.4 us -> 94.1 us
    pallas_call x1, Pallas kernels: 98.4 us -> 94.1 us  [on_device(): pl.pallas_call(functools.partial(kernel, n, nx), out_shape=jax.ShapeDtype...]
where the time goes in v4:
time: 95.4 us; the launch traced here: 95.2 us
  Pallas kernels  94.1 us (99%)
  local copies, waits for them, and re-layouts  1.1 us (1%)
    pallas_call x1, Pallas kernels, on_device(): pl.pallas_call(functools.partial(kernel, n, nx), out_shape=jax.ShapeDtype...  94.1 us

profile of v4, /device:TPU:1, one launch (start us, length us, event | category | flops | bytes accessed | tf_op | source)
XLA Modules:
  0.0 95.2 jit_solution(11512872478222569571)
XLA Ops:
  0.0 94.1 %shard_map.82 = f32[1,128]{1,0:T(1,128)} custom-call(bf16[128,1024]{1,0:T(8,128)(2,1)} %tok_in.1, bf16[8,512]{1,0:T(8,128)(2,1)} %w_up_in.1, bf16[8,512]{1,0:T(8,128)(2,1)} %bitcast.4, bf16[512]{0:T(512)(128)(2,1)} %bias_in.1, f32[1,1024]{1,0:T(1,128)} %bitcast.5, s32[1,16]{1,0:T(1,128)} %lengths_in.1, bf16[112,1024]{1,0:T(8,128)(2,1)} %pool_in.1, ...), custom_call_target="tpu_custom_call" | custom-call | tf_op jit(solution)/shard_map/pallas_call | solution.py:458
  94.1 0.0 copy-start
  94.1 0.6 copy-done
  94.7 0.5 copy.10
Async XLA Ops:
  94.1 0.6 copy-start

commit v5 on v4

--- a/solution.py
+++ b/solution.py
@@ -177,6 +177,30 @@
     G[c, 0, y, z] = shard[0]
     G[c, 1, z, y] = shard[1]
 
+    @pl.loop(1, n)
+    def _(k):
+        for h in range(2):
+            mine = (z, y)[h]
+            other = (mine + k) % n
+            slot_ = G.at[c, 0, y, other] if h == 0 else G.at[c, 1, z, other]
+            remote(shard.at[h], slot_, p1s.at[h, other], p1r.at[h, other], first[h](other)).wait_recv()
+
+    def second_hop(h, k):
+        q = place[h]
+        other = (q + k) % n
+        return remote(G.at[c, h, q], G.at[c, h, q], ws.at[h, other], wr.at[h, q], ring[h](other))
+
+    def to_sibling(h, i):
+        return remote(G.at[c, h, i], G.at[c, h, i], sibs.at[h, i], sibr.at[h, i], sibling)
+
+    @pl.loop(1, n)
+    def _(k):
+        second_hop(0, k).start()
+        second_hop(1, k).start()
+
+    to_sibling(0, y).start()
+    to_sibling(1, z).start()
+
     loads[3].wait()
     owner, place_in, label_col = slots(ids, n)
     slot = iota((total, rows), 0)
@@ -203,71 +227,58 @@
     rest = mod(o, m)
     from_ = mod(div(rest, 8), 2) * m + div(rest, 16) * 16 + div(o, m) * 8 + mod(rest, 8)
     order = jnp.where(i_ == from_, 1.0, 0.0).astype(BF16)
-
-    @pl.loop(1, n)
-    def _(k):
-        for h in range(2):
-            mine = (z, y)[h]
-            other = (mine + k) % n
-            slot_ = G.at[c, 0, y, other] if h == 0 else G.at[c, 1, z, other]
-            remote(shard.at[h], slot_, p1s.at[h, other], p1r.at[h, other], first[h](other)).wait_recv()
-
-    def second_hop(h, k):
-        q = place[h]
-        other = (q + k) % n
-        return remote(G.at[c, h, q], G.at[c, h, q], ws.at[h, other], wr.at[h, q], ring[h](other))
-
-    def to_sibling(h, i):
-        return remote(G.at[c, h, i], G.at[c, h, i], sibs.at[h, i], sibr.at[h, i], sibling)
-
-    @pl.loop(1, n)
-    def _(k):
-        second_hop(0, k).start()
-        second_hop(1, k).start()
-
     lab_y[0]()
-    to_sibling(0, y).start()
-    to_sibling(1, z).start()
 
     for load in loads[4:]:
         load.wait()
     pool_n = pool.shape[0]
     emb[0:pool_n, :] = unit_rows(pool[...].astype(F32))
 
-
     def pass_on(h, other):
         g = G.at[c, h, other]
         remote(g, g, ws.at[h, other], wr.at[h, other], ring[h](other)).wait_recv()
         to_sibling(h, other).start()
 
-    @pl.loop(1, n // 2)
-    def _(k):
+    def arrange(h, i):
+        g = G.at[1 - c, h, i]
+        remote(g, g, sibs.at[h, i], sibr.at[h, i], sibling).wait_recv()
+        pair = jnp.concatenate([G[0, h, i].reshape(m, hh), G[1, h, i].reshape(m, hh)], axis=0)
+        w = mm(order, pair).astype(BF16)
+        cols = slice(h * hh, (h + 1) * hh)
+        for ref, part in ((up, w[:m]), (down, w[m:])):
+            if h == 0:
+                for zz in range(n):
+                    at = pl.multiple_of((zz * n + i) * 16, 16)
+                    ref[pl.ds(at, 16), cols] = part[zz * 16 : (zz + 1) * 16]
+            else:
+                ref[pl.ds(pl.multiple_of(i * m, m), m), cols] = part
+
+    def arrange_at(k):
+        for h in range(2):
+            arrange(h, (place[h] + k) % n)
+            arrange(h, (place[h] + n - k) % n)
+
+    def pass_on_at(k):
         for h in range(2):
             pass_on(h, (place[h] + k) % n)
             pass_on(h, (place[h] + n - k) % n)
 
+    if n > 2:
+        pass_on_at(1)
+    arrange(0, y)
+    arrange(1, z)
+
+    @pl.loop(2, n // 2)
+    def _(k):
+        pass_on_at(k)
+        arrange_at(k - 1)
+
     for h in range(2):
         pass_on(h, (place[h] + n // 2) % n)
-
-    @pl.loop(0, n)
-    def _(i):
-        for h in range(2):
-            g = G.at[1 - c, h, i]
-            remote(g, g, sibs.at[h, i], sibr.at[h, i], sibling).wait_recv()
-
-    @pl.loop(0, n)
-    def _(i):
-        for h in range(2):
-            pair = jnp.concatenate([G[0, h, i].reshape(m, hh), G[1, h, i].reshape(m, hh)], axis=0)
-            w = mm(order, pair).astype(BF16)
-            cols = slice(h * hh, (h + 1) * hh)
-            for ref, part in ((up, w[:m]), (down, w[m:])):
-                if h == 0:
-                    for zz in range(n):
-                        at = pl.multiple_of((zz * n + i) * 16, 16)
-                        ref[pl.ds(at, 16), cols] = part[zz * 16 : (zz + 1) * 16]
-                else:
-                    ref[pl.ds(pl.multiple_of(i * m, m), m), cols] = part
+    if n > 2:
+        arrange_at(n // 2 - 1)
+    for h in range(2):
+        arrange(h, (place[h] + n // 2) % n)
 
     def ffn(block):
         pre = mm(block, up[...]) + bias[...].astype(F32).reshape(1, up.shape[1])
@@ -415,7 +426,8 @@
     v0 = jnp.sum(jnp.where(lane == yc * 2, got, 0.0), axis=1, keepdims=True)
     v1 = jnp.sum(jnp.where(lane == yc * 2 + 1, got, 0.0), axis=1, keepdims=True)
     mine = iota((dp, rows), 0) == owner_at
-    out[...] = jnp.sum(jnp.where(mine, jnp.where(place_in == 0, v0, v1), 0.0), axis=0, keepdims=True)
+    mine_best = jnp.where(mine, jnp.where(place_in == 0, v0, v1), 0.0)
+    out[...] = jnp.sum(mine_best, axis=0, keepdims=True).reshape(rows)
 
     @pl.loop(1, n)
     def _(k):
@@ -455,9 +467,9 @@
     def two(*shape):
         return [pltpu.SemaphoreType.DMA(shape)] * 2
 
-    out = pl.pallas_call(
+    return pl.pallas_call(
         functools.partial(kernel, n, nx),
-        out_shape=jax.ShapeDtypeStruct((1, rows), F32),
+        out_shape=jax.ShapeDtypeStruct((rows,), F32),
         in_specs=[ANY] * 8,
         out_specs=pl.BlockSpec(memory_space=pltpu.VMEM),
         scratch_shapes=[
@@ -527,7 +539,6 @@
         pool_rows,
         cluster_ids.reshape(1, rows),
     )
-    return out.reshape(rows)
 
 
 def solution(mesh):

time: 95.4 us -> 95 us (level)
  no operation moved by 1% of the time
where the time goes in v5:
time: 95 us; the launch traced here: 94.8 us
  Pallas kernels  93.6 us (99%)
  local copies, waits for them, and re-layouts  1.19 us (1%)
    pallas_call x1, Pallas kernels, on_device(): pl.pallas_call(functools.partial(kernel, n, nx), out_shape=jax.ShapeDtype...  93.6 us

profile of v5, /device:TPU:1, one launch (start us, length us, event | category | flops | bytes accessed | tf_op | source)
XLA Modules:
  0.0 94.8 jit_solution(2281671254970924967)
XLA Ops:
  0.0 93.6 %shard_map.82 = f32[128]{0:T(128)} custom-call(bf16[128,1024]{1,0:T(8,128)(2,1)} %tok_in.1, bf16[8,512]{1,0:T(8,128)(2,1)} %w_up_in.1, bf16[8,512]{1,0:T(8,128)(2,1)} %bitcast.3, bf16[512]{0:T(512)(128)(2,1)} %bias_in.1, f32[1,1024]{1,0:T(1,128)} %bitcast.4, s32[1,16]{1,0:T(1,128)} %lengths_in.1, bf16[112,1024]{1,0:T(8,128)(2,1)} %pool_in.1, s32[1,128]{1,0:T(1,128)} %bitcast.5), custom_call_target="tpu_custom_call" | custom-call | tf_op jit(solution)/shard_map/pallas_call | solution.py:470
  93.6 1.2 %copy.10 = f32[128]{0:T(128)} copy(f32[128]{0:T(128)} %shard_map.82) | data formatting | bytes 1024

commit v6 on v5

--- a/solution.py
+++ b/solution.py
@@ -77,13 +77,21 @@
 
         dst[mine] = src[...] if spread else src[mine]
 
-    def wait():
+    def landing(k):
+        other = (mine + k) % count
+        return remote(piece(other), dst.at[other], send.at[other], recv.at[other], dev(other))
+
+    def arrived():
         @pl.loop(1, count)
         def _(k):
-            other = (mine + k) % count
-            remote(piece(other), dst.at[other], send.at[other], recv.at[other], dev(other)).wait()
-
-    return start, wait
+            landing(k).wait_recv()
+
+    def sent():
+        @pl.loop(1, count)
+        def _(k):
+            landing(k).wait_send()
+
+    return start, arrived, sent
 
 
 def kernel(
@@ -301,22 +309,25 @@
     t_send[1].wait_recv()
     right = ffn(T[1])
     PS[1, hi] = right[half:].astype(BF16)
-    give(1, hi, RA.at[0, hi], xp)
     t_send[0].wait_recv()
     left = ffn(T[0])
     PS[0, lo] = left[:half].astype(BF16)
+    sums[0].wait_send()
+    sums[1].wait_send()
+    give(1, hi, RA.at[0, hi], xp)
     give(0, lo, RA.at[1, lo], xm)
-    lab_y[1]()
-    TL[...] = mm(by_z, RL[...].reshape(total, LAB)).astype(BF16).reshape(n, 2 * nyc, LAB)
-    lab_z[0]()
-
+    state = tok[...].astype(F32) + ffn(tok[...])
     sums[0].wait_recv()
     PS[1, lo] = (right[:half] + RF[0].astype(F32)).astype(BF16)
     give(1, lo, RA.at[0, lo], xp)
     sums[1].wait_recv()
     PS[0, hi] = (left[half:] + RF[1].astype(F32)).astype(BF16)
     give(0, hi, RA.at[1, hi], xm)
-    state = tok[...].astype(F32) + ffn(tok[...])
+
+    lab_y[1]()
+    TL[...] = mm(by_z, RL[...].reshape(total, LAB)).astype(BF16).reshape(n, 2 * nyc, LAB)
+    lab_z[0]()
+
     for q in sums[2:]:
         q.wait_recv()
     state = state + RA[0].astype(F32) + RA[1].astype(F32)
@@ -346,10 +357,13 @@
     for k in range(2):
         e0 = emb[:, 2 * k * w : (2 * k + 1) * w]
         e1 = emb[:, (2 * k + 1) * w : (2 * k + 2) * w]
+        SQ[k] = mm(pick1, e1).astype(BF16).reshape(n, 2 * nyc, w)
         SP[k] = mm(pick0, e0).astype(BF16).reshape(nyc, 2 * n, w)
+        if k:
+            q_z[0][2]()
+            p_y[0][2]()
+        q_z[k][0]()
         p_y[k][0]()
-        SQ[k] = mm(pick1, e1).astype(BF16).reshape(n, 2 * nyc, w)
-        q_z[k][0]()
     lab_z[1]()
     lx = [
         remote(L.at[0], L.at[1], lxs.at[0], lxr.at[0], (me, xp)),
@@ -358,12 +372,12 @@
     for t in lx:
         t.start()
     for k in range(2):
+        q_z[k][1]()
+        TQ[k] = mm(by_yc, RQ[k].reshape(total, w)).astype(BF16).reshape(nyc, 2 * n, w)
+        q_y[k][0]()
         p_y[k][1]()
         TP[k] = mm(by_z, RP[k].reshape(total, w)).astype(BF16).reshape(n, 2 * nyc, w)
         p_z[k][0]()
-        q_z[k][1]()
-        TQ[k] = mm(by_yc, RQ[k].reshape(total, w)).astype(BF16).reshape(nyc, 2 * n, w)
-        q_y[k][0]()
 
     xs = []
     for k in range(2):
@@ -440,8 +454,10 @@
         to_sibling(0, i).wait_send()
         to_sibling(1, i).wait_send()
 
-    for t in [*t_send, *sums, *lx, *xs]:
+    for t in [*t_send, *sums[2:], *lx, *xs]:
         t.wait_send()
+    for hop in (lab_y, lab_z, q_z[1], p_y[1], *q_y, *p_z, back_z, back_y):
+        hop[2]()
 
 
 ANY = pl.BlockSpec(memory_space=pl.ANY)

time: 95 us -> 95.2 us (level)
  no operation moved by 1% of the time
where the time goes in v6:
time: 95.2 us; the launch traced here: 95 us
  Pallas kernels  93.8 us (99%)
  local copies, waits for them, and re-layouts  1.19 us (1%)
    pallas_call x1, Pallas kernels, on_device(): pl.pallas_call(functools.partial(kernel, n, nx), out_shape=jax.ShapeDtype...  93.8 us

profile of v6, /device:TPU:1, one launch (start us, length us, event | category | flops | bytes accessed | tf_op | source)
XLA Modules:
  0.0 95.0 jit_solution(4293384296351267383)
XLA Ops:
  0.0 93.8 %shard_map.82 = f32[128]{0:T(128)} custom-call(bf16[128,1024]{1,0:T(8,128)(2,1)} %tok_in.1, bf16[8,512]{1,0:T(8,128)(2,1)} %w_up_in.1, bf16[8,512]{1,0:T(8,128)(2,1)} %bitcast.3, bf16[512]{0:T(512)(128)(2,1)} %bias_in.1, f32[1,1024]{1,0:T(1,128)} %bitcast.4, s32[1,16]{1,0:T(1,128)} %lengths_in.1, bf16[112,1024]{1,0:T(8,128)(2,1)} %pool_in.1, s32[1,128]{1,0:T(1,128)} %bitcast.5), custom_call_target="tpu_custom_call" | custom-call | tf_op jit(solution)/shard_map/pallas_call | solution.py:486
  93.8 1.2 %copy.10 = f32[128]{0:T(128)} copy(f32[128]{0:T(128)} %shard_map.82) | data formatting | bytes 1024

commit v7 on v6

--- a/solution.py
+++ b/solution.py
@@ -11,6 +11,8 @@
 MESH = pl.DeviceIdType.MESH
 F32, BF16 = jnp.float32, jnp.bfloat16
 LAB = 128
+KC = 4
+NP = 4
 
 
 def iota(shape, dim):
@@ -185,30 +187,6 @@
     G[c, 0, y, z] = shard[0]
     G[c, 1, z, y] = shard[1]
 
-    @pl.loop(1, n)
-    def _(k):
-        for h in range(2):
-            mine = (z, y)[h]
-            other = (mine + k) % n
-            slot_ = G.at[c, 0, y, other] if h == 0 else G.at[c, 1, z, other]
-            remote(shard.at[h], slot_, p1s.at[h, other], p1r.at[h, other], first[h](other)).wait_recv()
-
-    def second_hop(h, k):
-        q = place[h]
-        other = (q + k) % n
-        return remote(G.at[c, h, q], G.at[c, h, q], ws.at[h, other], wr.at[h, q], ring[h](other))
-
-    def to_sibling(h, i):
-        return remote(G.at[c, h, i], G.at[c, h, i], sibs.at[h, i], sibr.at[h, i], sibling)
-
-    @pl.loop(1, n)
-    def _(k):
-        second_hop(0, k).start()
-        second_hop(1, k).start()
-
-    to_sibling(0, y).start()
-    to_sibling(1, z).start()
-
     loads[3].wait()
     owner, place_in, label_col = slots(ids, n)
     slot = iota((total, rows), 0)
@@ -235,17 +213,38 @@
     rest = mod(o, m)
     from_ = mod(div(rest, 8), 2) * m + div(rest, 16) * 16 + div(o, m) * 8 + mod(rest, 8)
     order = jnp.where(i_ == from_, 1.0, 0.0).astype(BF16)
-    lab_y[0]()
-
-    for load in loads[4:]:
-        load.wait()
-    pool_n = pool.shape[0]
-    emb[0:pool_n, :] = unit_rows(pool[...].astype(F32))
-
-    def pass_on(h, other):
-        g = G.at[c, h, other]
-        remote(g, g, ws.at[h, other], wr.at[h, other], ring[h](other)).wait_recv()
-        to_sibling(h, other).start()
+
+    @pl.loop(1, n)
+    def _(k):
+        for h in range(2):
+            mine = (z, y)[h]
+            other = (mine + k) % n
+            slot_ = G.at[c, 0, y, other] if h == 0 else G.at[c, 1, z, other]
+            remote(shard.at[h], slot_, p1s.at[h, other], p1r.at[h, other], first[h](other)).wait_recv()
+
+    def hop_of(h, row_, part_, sem, to):
+        r = G.at[c, h, row_] if part_ is None else G.at[c, h, row_, pl.ds(part_ * (n // 2), n // 2)]
+        rs = wr.at[h, n] if part_ == 1 else wr.at[h, row_]
+        return remote(r, r, ws.at[h, sem], rs, ring[h](to))
+
+    def around(h, k):
+        return (place[h] + n + k) % n
+
+    hops = []
+
+    def go(h, row_, part_, sem, to):
+        hops.append(hop_of(h, around(h, row_), part_, sem, around(h, to)))
+        hops[-1].start()
+
+    def to_sibling(h, i):
+        return remote(G.at[c, h, i], G.at[c, h, i], sibs.at[h, i], sibr.at[h, i], sibling)
+
+    for h in range(2):
+        for k_, to in enumerate((2, -2, 1, -1)):
+            go(h, 0, None, k_, to)
+
+    to_sibling(0, y).start()
+    to_sibling(1, z).start()
 
     def arrange(h, i):
         g = G.at[1 - c, h, i]
@@ -266,27 +265,45 @@
             arrange(h, (place[h] + k) % n)
             arrange(h, (place[h] + n - k) % n)
 
-    def pass_on_at(k):
-        for h in range(2):
-            pass_on(h, (place[h] + k) % n)
-            pass_on(h, (place[h] + n - k) % n)
-
-    if n > 2:
-        pass_on_at(1)
+    def got(h, row_, part_=None):
+        hop_of(h, around(h, row_), part_, 0, around(h, row_)).wait_recv()
+
+    for h in range(2):
+        got(h, -1)
+        go(h, -1, None, 4, 2)
+        got(h, 1)
+        go(h, 1, None, 5, -2)
+    for h in range(2):
+        got(h, -2)
+        go(h, -2, 0, 6, 2)
+        got(h, 2)
+        go(h, 2, 1, 7, -2)
+    for h in range(2):
+        for k in (1, -1, 2, -2):
+            to_sibling(h, around(h, k)).start()
+
+    lab_y[0]()
+
+    for load in loads[4:]:
+        load.wait()
+    pool_n = pool.shape[0]
+    emb[0:pool_n, :] = unit_rows(pool[...].astype(F32))
+
     arrange(0, y)
     arrange(1, z)
-
-    @pl.loop(2, n // 2)
-    def _(k):
-        pass_on_at(k)
-        arrange_at(k - 1)
-
+    arrange_at(1)
+    arrange_at(2)
     for h in range(2):
-        pass_on(h, (place[h] + n // 2) % n)
-    if n > 2:
-        arrange_at(n // 2 - 1)
+        for k in (3, -3):
+            got(h, k)
+            to_sibling(h, around(h, k)).start()
     for h in range(2):
-        arrange(h, (place[h] + n // 2) % n)
+        got(h, n // 2, 0)
+        got(h, n // 2, 1)
+        to_sibling(h, around(h, n // 2)).start()
+    arrange_at(3)
+    for h in range(2):
+        arrange(h, around(h, n // 2))
 
     def ffn(block):
         pre = mm(block, up[...]) + bias[...].astype(F32).reshape(1, up.shape[1])
@@ -294,41 +311,47 @@
         return mm_nt(hidden, down[...])
 
     half = toks // 2
-    lo, hi = pl.ds(0, half), pl.ds(half, half)
-    sums = []
+    size = half // NP
+    lo = [pl.ds(k * size, size) for k in range(NP)]
+    hi = [pl.ds(half + k * size, size) for k in range(NP)]
+    low, high = pl.ds(0, half), pl.ds(half, half)
+    sums, final = [], []
 
     def give(j, rows_, dst, to):
         k = len(sums)
         sums.append(remote(PS.at[j, rows_], dst, qs.at[k], qr.at[k], (me, to)))
         sums[-1].start()
+        return sums[-1]
 
     t_send[2].wait_recv()
     PS[2] = ffn(T[2]).astype(BF16)
-    give(2, lo, RF.at[0], xp)
-    give(2, hi, RF.at[1], xm)
+    on_p, on_m = [], []
+    for k in range(NP):
+        on_p.append(give(2, lo[k], RF.at[0, lo[k]], xp))
+        on_m.append(give(2, hi[k], RF.at[1, lo[k]], xm))
     t_send[1].wait_recv()
     right = ffn(T[1])
-    PS[1, hi] = right[half:].astype(BF16)
     t_send[0].wait_recv()
     left = ffn(T[0])
-    PS[0, lo] = left[:half].astype(BF16)
-    sums[0].wait_send()
-    sums[1].wait_send()
-    give(1, hi, RA.at[0, hi], xp)
-    give(0, lo, RA.at[1, lo], xm)
+    PS[1, high] = right[half:].astype(BF16)
+    PS[0, low] = left[:half].astype(BF16)
+    final.append(give(1, high, RA.at[0, high], xp))
+    final.append(give(0, low, RA.at[1, low], xm))
     state = tok[...].astype(F32) + ffn(tok[...])
-    sums[0].wait_recv()
-    PS[1, lo] = (right[:half] + RF[0].astype(F32)).astype(BF16)
-    give(1, lo, RA.at[0, lo], xp)
-    sums[1].wait_recv()
-    PS[0, hi] = (left[half:] + RF[1].astype(F32)).astype(BF16)
-    give(0, hi, RA.at[1, hi], xm)
+    for k in range(NP):
+        a, b = k * size, half + k * size
+        on_p[k].wait_recv()
+        PS[1, lo[k]] = (right[a : a + size] + RF[0, lo[k]].astype(F32)).astype(BF16)
+        final.append(give(1, lo[k], RA.at[0, lo[k]], xp))
+        on_m[k].wait_recv()
+        PS[0, hi[k]] = (left[b : b + size] + RF[1, lo[k]].astype(F32)).astype(BF16)
+        final.append(give(0, hi[k], RA.at[1, hi[k]], xm))
 
     lab_y[1]()
     TL[...] = mm(by_z, RL[...].reshape(total, LAB)).astype(BF16).reshape(n, 2 * nyc, LAB)
     lab_z[0]()
 
-    for q in sums[2:]:
+    for q in final:
         q.wait_recv()
     state = state + RA[0].astype(F32) + RA[1].astype(F32)
 
@@ -349,19 +372,16 @@
     )
     emb[pool_n : pool_n + docs, :] = unit_rows(pooled)
 
-    w = d // 4
-    p_y = [exchange(SP.at[k], RP.at[k], yc, nyc, at_yc, yps.at[k], ypr.at[k]) for k in range(2)]
-    p_z = [exchange(TP.at[k], FP.at[k], z, n, at_z, zps.at[k], zpr.at[k]) for k in range(2)]
-    q_z = [exchange(SQ.at[k], RQ.at[k], z, n, at_z, zqs.at[k], zqr.at[k]) for k in range(2)]
-    q_y = [exchange(TQ.at[k], FQ.at[k], yc, nyc, at_yc, yqs.at[k], yqr.at[k]) for k in range(2)]
-    for k in range(2):
+    w = d // (2 * KC)
+    p_y = [exchange(SP.at[k], RP.at[k], yc, nyc, at_yc, yps.at[k], ypr.at[k]) for k in range(KC)]
+    p_z = [exchange(TP.at[k], FP.at[k], z, n, at_z, zps.at[k], zpr.at[k]) for k in range(KC)]
+    q_z = [exchange(SQ.at[k], RQ.at[k], z, n, at_z, zqs.at[k], zqr.at[k]) for k in range(KC)]
+    q_y = [exchange(TQ.at[k], FQ.at[k], yc, nyc, at_yc, yqs.at[k], yqr.at[k]) for k in range(KC)]
+    for k in range(KC):
         e0 = emb[:, 2 * k * w : (2 * k + 1) * w]
         e1 = emb[:, (2 * k + 1) * w : (2 * k + 2) * w]
         SQ[k] = mm(pick1, e1).astype(BF16).reshape(n, 2 * nyc, w)
         SP[k] = mm(pick0, e0).astype(BF16).reshape(nyc, 2 * n, w)
-        if k:
-            q_z[0][2]()
-            p_y[0][2]()
         q_z[k][0]()
         p_y[k][0]()
     lab_z[1]()
@@ -371,7 +391,7 @@
     ]
     for t in lx:
         t.start()
-    for k in range(2):
+    for k in range(KC):
         q_z[k][1]()
         TQ[k] = mm(by_yc, RQ[k].reshape(total, w)).astype(BF16).reshape(nyc, 2 * n, w)
         q_y[k][0]()
@@ -380,7 +400,7 @@
         p_z[k][0]()
 
     xs = []
-    for k in range(2):
+    for k in range(KC):
         p_z[k][1]()
         E[0, k, :, :w] = FP[k].reshape(total, w)
         q_y[k][1]()
@@ -405,21 +425,24 @@
     def best_of(sc, keep):
         return jnp.max(jnp.where(keep, sc, -1.0), axis=0, keepdims=True)
 
-    best = best_of(part(0, 0, 0) + part(0, 0, 1), (col0 == row0) & ~eye)
-    xs[0].wait_recv()
-    xs[1].wait_recv()
-    s21, s10, s20 = part(2, 1, 0), part(1, 0, 0), part(2, 0, 0)
-    xs[2].wait_recv()
-    xs[3].wait_recv()
-    B1[1] = jnp.broadcast_to(best_of(s21 + part(2, 1, 1), col2 == row1), B1.shape[1:])
+    best = best_of(sum(part(0, 0, k) for k in range(KC)), (col0 == row0) & ~eye)
+    s21, s10, s20 = [], [], []
+    for k in range(KC):
+        xs[2 * k].wait_recv()
+        xs[2 * k + 1].wait_recv()
+        s21.append(part(2, 1, k))
+        if k < KC - 1:
+            s10.append(part(1, 0, k))
+            s20.append(part(2, 0, k))
+    B1[1] = jnp.broadcast_to(best_of(sum(s21), col2 == row1), B1.shape[1:])
     over = B1.at[1, pl.ds(0, 1)]
 
     @pl.loop(0, n)
     def _(zz):
         remote(over, BM.at[z], bms.at[zz], bmr.at[z], (zz * nyc + yc, xm)).start()
 
-    best = jnp.maximum(best, best_of(s10 + part(1, 0, 1), col1 == row0))
-    best = jnp.maximum(best, best_of(s20 + part(2, 0, 1), col2 == row0))
+    best = jnp.maximum(best, best_of(sum(s10) + part(1, 0, KC - 1), col1 == row0))
+    best = jnp.maximum(best, best_of(sum(s20) + part(2, 0, KC - 1), col2 == row0))
     B1[0] = jnp.broadcast_to(best, B1.shape[1:])
 
     back_z = exchange(B1.at[0, pl.ds(0, 1)], B2, z, n, at_z, b1s, b1r, spread=True)
@@ -447,16 +470,15 @@
     def _(k):
         for h in range(2):
             first_hop(h, k).wait_send()
-            second_hop(h, k).wait_send()
 
     @pl.loop(0, n)
     def _(i):
         to_sibling(0, i).wait_send()
         to_sibling(1, i).wait_send()
 
-    for t in [*t_send, *sums[2:], *lx, *xs]:
+    for t in [*hops, *t_send, *sums, *lx, *xs]:
         t.wait_send()
-    for hop in (lab_y, lab_z, q_z[1], p_y[1], *q_y, *p_z, back_z, back_y):
+    for hop in (lab_y, lab_z, *q_z, *p_y, *q_y, *p_z, back_z, back_y):
         hop[2]()
 
 
@@ -471,7 +493,7 @@
     nyc = 2 * n
     dp = nyc * n
     total = 2 * dp
-    w = d // 4
+    w = d // (2 * KC)
     keep = min(total, 128)
 
     def vm(*shape):
@@ -510,15 +532,15 @@
             vm(nyc, 2 * n, LAB),
             vm(n, 2 * nyc, LAB),
             vm(3, n, 2 * nyc, LAB),
-            vm(2, nyc, 2 * n, w),
-            vm(2, nyc, 2 * n, w),
-            vm(2, n, 2 * nyc, w),
-            vm(2, n, 2 * nyc, w),
-            vm(2, n, 2 * nyc, w),
-            vm(2, n, 2 * nyc, w),
-            vm(2, nyc, 2 * n, w),
-            vm(2, nyc, 2 * n, w),
-            vm(3, 2, total, 2 * w),
+            vm(KC, nyc, 2 * n, w),
+            vm(KC, nyc, 2 * n, w),
+            vm(KC, n, 2 * nyc, w),
+            vm(KC, n, 2 * nyc, w),
+            vm(KC, n, 2 * nyc, w),
+            vm(KC, n, 2 * nyc, w),
+            vm(KC, nyc, 2 * n, w),
+            vm(KC, nyc, 2 * n, w),
+            vm(3, KC, total, 2 * w),
             vf(2, 8, total),
             vf(n, 1, total),
             vf(n, 1, total),
@@ -526,18 +548,18 @@
             vf(nyc, n, keep),
             pltpu.SemaphoreType.DMA((8,)),
             *two(2, n),
-            *two(2, n),
+            *two(2, n + 1),
             *two(2, n),
             *two(3),
-            *two(6),
+            *two(2 + 4 * NP),
             *two(nyc),
             *two(n),
             *two(2),
-            *two(2, nyc),
-            *two(2, n),
-            *two(2, n),
-            *two(2, nyc),
-            *two(2, 2),
+            *two(KC, nyc),
+            *two(KC, n),
+            *two(KC, n),
+            *two(KC, nyc),
+            *two(2, KC),
             *two(n),
             *two(n),
             *two(nyc),

time: 95.2 us -> 93.1 us (0.978)
  Pallas kernels: 93.8 us -> 91.8 us
    pallas_call x1, Pallas kernels: 93.8 us -> 91.8 us  [on_device(): pl.pallas_call(functools.partial(kernel, n, nx), out_shape=jax.ShapeDtype...]
where the time goes in v7:
time: 93.1 us; the launch traced here: 93 us
  Pallas kernels  91.8 us (99%)
  local copies, waits for them, and re-layouts  1.19 us (1%)
    pallas_call x1, Pallas kernels, on_device(): pl.pallas_call(functools.partial(kernel, n, nx), out_shape=jax.ShapeDtype...  91.8 us

profile of v7, /device:TPU:1, one launch (start us, length us, event | category | flops | bytes accessed | tf_op | source)
XLA Modules:
  0.0 93.0 jit_solution(2075186004430888821)
XLA Ops:
  0.0 91.8 %shard_map.82 = f32[128]{0:T(128)} custom-call(bf16[128,1024]{1,0:T(8,128)(2,1)} %tok_in.1, bf16[8,512]{1,0:T(8,128)(2,1)} %w_up_in.1, bf16[8,512]{1,0:T(8,128)(2,1)} %bitcast.3, bf16[512]{0:T(512)(128)(2,1)} %bias_in.1, f32[1,1024]{1,0:T(1,128)} %bitcast.4, s32[1,16]{1,0:T(1,128)} %lengths_in.1, bf16[112,1024]{1,0:T(8,128)(2,1)} %pool_in.1, s32[1,128]{1,0:T(1,128)} %bitcast.5), custom_call_target="tpu_custom_call" | custom-call | tf_op jit(solution)/shard_map/pallas_call | solution.py:508
  91.8 1.2 %copy.10 = f32[128]{0:T(128)} copy(f32[128]{0:T(128)} %shard_map.82) | data formatting | bytes 1024

commit v8 on v7

--- a/solution.py
+++ b/solution.py
@@ -291,8 +291,6 @@
 
     arrange(0, y)
     arrange(1, z)
-    arrange_at(1)
-    arrange_at(2)
     for h in range(2):
         for k in (3, -3):
             got(h, k)
@@ -301,6 +299,8 @@
         got(h, n // 2, 0)
         got(h, n // 2, 1)
         to_sibling(h, around(h, n // 2)).start()
+    arrange_at(1)
+    arrange_at(2)
     arrange_at(3)
     for h in range(2):
         arrange(h, around(h, n // 2))

time: 93.1 us -> 92.9 us (level)
  no operation moved by 1% of the time
where the time goes in v8:
time: 92.9 us; the launch traced here: 92.7 us
  Pallas kernels  91.5 us (98%)
  local copies, waits for them, and re-layouts  1.19 us (1%)
    pallas_call x1, Pallas kernels, on_device(): pl.pallas_call(functools.partial(kernel, n, nx), out_shape=jax.ShapeDtype...  91.5 us

profile of v8, /device:TPU:1, one launch (start us, length us, event | category | flops | bytes accessed | tf_op | source)
XLA Modules:
  0.0 92.7 jit_solution(10429664761846516274)
XLA Ops:
  0.0 91.5 %shard_map.82 = f32[128]{0:T(128)} custom-call(bf16[128,1024]{1,0:T(8,128)(2,1)} %tok_in.1, bf16[8,512]{1,0:T(8,128)(2,1)} %w_up_in.1, bf16[8,512]{1,0:T(8,128)(2,1)} %bitcast.3, bf16[512]{0:T(512)(128)(2,1)} %bias_in.1, f32[1,1024]{1,0:T(1,128)} %bitcast.4, s32[1,16]{1,0:T(1,128)} %lengths_in.1, bf16[112,1024]{1,0:T(8,128)(2,1)} %pool_in.1, s32[1,128]{1,0:T(1,128)} %bitcast.5), custom_call_target="tpu_custom_call" | custom-call | tf_op jit(solution)/shard_map/pallas_call | solution.py:508
  91.5 1.2 %copy.10 = f32[128]{0:T(128)} copy(f32[128]{0:T(128)} %shard_map.82) | data formatting | bytes 1024
